TPU v7x, 32 devices: a whole 2x2x4 slice. The times are simulated.
32 devices in a mesh: gx: 8 (over y, x, core), gy: 4 (over z).
Axes of the slice: x: 2, y: 2, z: 4, core: 2. Of those that a mesh axis runs over, the one named last changes fastest.
Arguments:
- u_now: float32 [3, 6, 64, 512], P(None, None, 'gx', 'gy'), may hold values from -6 to 6
- u_prev: float32 [3, 6, 64, 512], P(None, None, 'gx', 'gy'), may hold values from -6 to 6
- lame_lambda: float32 [6, 64, 512], P(None, 'gx', 'gy'), may hold values from 0.5 to 1.5
- lame_mu: float32 [6, 64, 512], P(None, 'gx', 'gy'), may hold values from 0.3 to 1
- buoyancy: float32 [6, 64, 512], P(None, 'gx', 'gy'), may hold values from 0.5 to 1
- q_now: float32 [2048, 128], P(('gx', 'gy')), may hold values from -3 to 3
- q_prev: float32 [2048, 128], P(('gx', 'gy')), may hold values from -3 to 3
- archetype: int32 [2048], P(('gx', 'gy')), may hold values from 0 to 7
- stiffness: float32 [8, 128, 128], replicated, may hold values from -1.2 to 14, as said below
- couple: float32 [8, 3, 128], replicated, may hold values from -1.5 to 1.5
- counts: int32 [8, 4, 4], P('gx'), may hold values from 1 to 16, as said below
- footprint: int32 [8, 4, 256], P('gx', 'gy'), may hold values from 0 to 1023, as said below
Outputs:
- u_last: float32 [3, 6, 64, 512], P(None, None, 'gx', 'gy')
- u_before: float32 [3, 6, 64, 512], P(None, None, 'gx', 'gy')
- q_last: float32 [2048, 128], P(('gx', 'gy'))
- q_before: float32 [2048, 128], P(('gx', 'gy'))
Inputs may be any that keep to these rules, and one draw needn't show every extreme that they name: `stiffness`: symmetric, one matrix for each archetype. `counts`: at most 16; in every tile row some owner column receives 16 from every home column. `footprint`: the 4 cells of a slot form a 2 x 2 square of the home tile's surface, numbered x * 128 + y.
All inputs are finite; a program needn't handle non-finite values.
Results may differ from a plain program's by a relative error of at most 0.0001.
Values sent between devices are 32-bit elements; how exact they have to be, the bound alone decides.
A program may use at most 64 MiB of HBM per device.

v0:
```python
import functools

import jax
import jax.numpy as jnp
from jax import lax
from jax.experimental import pallas as pl
from jax.experimental.pallas import tpu as pltpu
from jax.sharding import PartitionSpec as P

FOOTPRINT_CELLS = 4
STEPS = 2
TIME_STEP = 0.25
RIM = 4
MESH = pl.DeviceIdType.MESH
F32 = jnp.float32
BF16 = jnp.bfloat16

X_DIRS = ((1, 0), (-1, 0))
Y_DIRS = ((-1, 1), (-1, -1), (0, 1), (0, -1), (1, 1), (1, -1))


def iota(shape, dim):
    return lax.broadcasted_iota(jnp.int32, shape, dim)


def split(value):
    high = value.astype(BF16)
    return high, (value - high.astype(F32)).astype(BF16)


def pack_x(fields):
    half = fields.shape[0] // 2
    first, second = fields[:half], fields[half:]
    upper = iota((1, 8, 128), 1) < RIM
    to_next = jnp.where(upper, pltpu.roll(first, RIM, 1), second)
    to_before = jnp.where(upper, first, pltpu.roll(second, RIM, 1))
    return to_next, to_before


def unpack_x(from_before, from_next):
    upper = iota((1, 8, 128), 1) < RIM
    first = jnp.where(upper, from_next, pltpu.roll(from_before, RIM, 1))
    second = jnp.where(upper, pltpu.roll(from_next, RIM, 1), from_before)
    return jnp.concatenate([first, second], axis=0)


def pack_y(fields):
    count = fields.shape[0]
    lane = iota((8, 128), 1)
    tiles = []
    for start in range(0, count, 16):
        tile = jnp.zeros((8, 128), F32)
        for k in range(start, min(start + 16, count)):
            place = 8 * (k - start)
            moved = pltpu.roll(fields[k], (place + RIM) % 128, 1)
            tile = jnp.where((lane >= place) & (lane < place + 8), moved, tile)
        tiles.append(tile)
    return jnp.stack(tiles)


def unpack_y(tiles, count):
    slabs = []
    for k in range(count):
        slabs.append(pltpu.roll(tiles[k // 16], (124 - 8 * (k % 16)) % 128, 1))
    return jnp.stack(slabs)


def slope(here, other, axis, both):
    size = here.shape[axis]
    place = iota((1,) * (here.ndim - 2) + (8, 128), axis)

    def shifted(mine, theirs, shift):
        entering = place < shift if shift > 0 else place >= size + shift
        return pltpu.roll(jnp.where(entering, theirs, mine), (-shift) % size, axis)

    def slope_of(mine, theirs):
        return 8.0 * (shifted(mine, theirs, 1) - shifted(mine, theirs, -1)) - (
            shifted(mine, theirs, 2) - shifted(mine, theirs, -2)
        )

    if both:
        return slope_of(here, other), slope_of(other, here)
    return slope_of(here, other)


def slope_z(field):
    nothing = jnp.zeros((2,) + field.shape[1:], F32)
    padded = jnp.concatenate([nothing, field, nothing], axis=0)
    n = field.shape[0]
    return 8.0 * (padded[3 : n + 3] - padded[1 : n + 1]) - (padded[4 : n + 4] - padded[:n])


def divergence(u, rim_x, rim_y, corner, lam, mu, lam_x, mu_x, lam_y, mu_y):
    ux, uy, uz = u[0], u[1], u[2]
    x_x, x_xh = slope(ux, rim_x[0], 1, True)
    y_x, y_xh = slope(uy, rim_x[1], 1, True)
    z_x, z_xh = slope(uz, rim_x[2], 1, True)
    x_y, x_yh = slope(ux, rim_y[0], 2, True)
    y_y, y_yh = slope(uy, rim_y[1], 2, True)
    z_y, z_yh = slope(uz, rim_y[2], 2, True)
    x_z, y_z, z_z = slope_z(ux), slope_z(uy), slope_z(uz)
    spread = lam * (x_x + y_y + z_z)
    s_xx = spread + 2.0 * mu * x_x
    s_yy = spread + 2.0 * mu * y_y
    s_zz = spread + 2.0 * mu * z_z
    s_xy = mu * (x_y + y_x)
    s_xz = mu * (x_z + z_x)
    s_yz = mu * (y_z + z_y)
    x_yr = slope(rim_x[0], corner[0], 2, False)
    y_yr = slope(rim_x[1], corner[1], 2, False)
    x_zr, z_zr = slope_z(rim_x[0]), slope_z(rim_x[2])
    s_xx_r = lam_x * (x_xh + y_yr + z_zr) + 2.0 * mu_x * x_xh
    s_xy_r = mu_x * (x_yr + y_xh)
    s_xz_r = mu_x * (x_zr + z_xh)
    x_xc = slope(rim_y[0], corner[0], 1, False)
    y_xc = slope(rim_y[1], corner[1], 1, False)
    y_zc, z_zc = slope_z(rim_y[1]), slope_z(rim_y[2])
    s_yy_c = lam_y * (x_xc + y_yh + z_zc) + 2.0 * mu_y * y_yh
    s_xy_c = mu_y * (x_yh + y_xc)
    s_yz_c = mu_y * (y_zc + z_yh)
    total_x = slope(s_xx, s_xx_r, 1, False) + slope(s_xy, s_xy_c, 2, False) + slope_z(s_xz)
    total_y = slope(s_xy, s_xy_r, 1, False) + slope(s_yy, s_yy_c, 2, False) + slope_z(s_yz)
    total_z = slope(s_xz, s_xz_r, 1, False) + slope(s_yz, s_yz_c, 2, False) + slope_z(s_zz)
    return jnp.stack([total_x, total_y, total_z])


def kernel(
    rows,
    owners,
    u_hbm,
    u_prev_hbm,
    lam_hbm,
    mu_hbm,
    buoy_hbm,
    q_hbm,
    q_prev_hbm,
    arch_hbm,
    stiff_hbm,
    couple_hbm,
    counts_hbm,
    cells_hbm,
    u_last_ref,
    u_before_ref,
    q_last_ref,
    q_before_ref,
    xs0,
    xs1,
    xr0,
    xr1,
    ys,
    yr,
    bs,
    br,
    table,
    u_ref,
    u_prev_ref,
    lam_ref,
    mu_ref,
    buoy_ref,
    q_ref,
    q_prev_ref,
    arch_ref,
    stiff_ref,
    couple_ref,
    counts_ref,
    cells_ref,
    loaded,
    x_send,
    x_recv,
    y_send,
    y_recv,
    b_send,
    b_recv,
):
    r, h = lax.axis_index("gx"), lax.axis_index("gy")
    nz = lam_ref.shape[0]
    slots = q_ref.shape[0]
    capacity = slots // owners
    kinds = stiff_ref.shape[0]
    freedoms = q_ref.shape[1]
    xs, xr = (xs0, xs1), (xr0, xr1)

    def target(direction):
        dx, dy = direction
        there = None
        for d, me, n in ((dx, r, rows), (dy, h, owners)):
            if d:
                ok = me + d < n if d > 0 else me > 0
                there = ok if there is None else there & ok
        return there, (r + dx, h + dy)

    def source(direction):
        return target((-direction[0], -direction[1]))

    peers = X_DIRS + tuple(d for d in Y_DIRS if d[0])

    barrier = pltpu.get_barrier_semaphore()
    arrivals = jnp.int32(owners - 1)
    for step in range(1, owners):
        other = lax.rem(h + step, owners)
        pl.semaphore_signal(barrier, inc=1, device_id=(r, other), device_id_type=MESH)

    for direction in peers:
        there, device = target(direction)
        arrivals = arrivals + there.astype(jnp.int32)

        @pl.when(there)
        def _(device=device):
            pl.semaphore_signal(barrier, inc=1, device_id=device, device_id_type=MESH)

    loads = {}
    for source_ref, ref in (
        (cells_hbm, cells_ref),
        (counts_hbm, counts_ref),
        (arch_hbm, arch_ref),
        (couple_hbm, couple_ref),
        (u_hbm, u_ref),
        (q_hbm, q_ref),
        (lam_hbm, lam_ref),
        (mu_hbm, mu_ref),
        (stiff_hbm, stiff_ref),
        (q_prev_hbm, q_prev_ref),
        (u_prev_hbm, u_prev_ref),
        (buoy_hbm, buoy_ref),
    ):
        copy = pltpu.make_async_copy(source_ref, ref, loaded.at[len(loads)])
        copy.start()
        loads[id(ref)] = copy

    for slot, direction in enumerate(X_DIRS):
        there, _ = source(direction)

        @pl.when(jnp.logical_not(there))
        def _(slot=slot):
            for buffer in xr:
                buffer[slot] = jnp.zeros(buffer.shape[1:], F32)

    for slot, direction in enumerate(Y_DIRS):
        there, _ = source(direction)

        @pl.when(jnp.logical_not(there))
        def _(slot=slot):
            for turn in range(STEPS):
                yr[turn, slot] = jnp.zeros(yr.shape[2:], F32)

    def load(ref):
        loads[id(ref)].wait()
        return ref[...]

    def x_copy(turn, slot, device):
        return pltpu.make_async_remote_copy(
            src_ref=xs[turn].at[slot],
            dst_ref=xr[turn].at[slot],
            send_sem=x_send.at[turn, slot],
            recv_sem=x_recv.at[turn, slot],
            device_id=device,
            device_id_type=MESH,
        )

    def y_copy(turn, slot, device):
        return pltpu.make_async_remote_copy(
            src_ref=ys.at[turn],
            dst_ref=yr.at[turn, slot],
            send_sem=y_send.at[turn, slot],
            recv_sem=y_recv.at[turn, slot],
            device_id=device,
            device_id_type=MESH,
        )

    def b_copy(turn, step):
        other = lax.rem(h + step, owners)
        return pltpu.make_async_remote_copy(
            src_ref=bs.at[turn, other],
            dst_ref=br.at[turn, h],
            send_sem=b_send.at[turn, step],
            recv_sem=b_recv.at[turn, step],
            device_id=(r, other),
            device_id_type=MESH,
        )

    def b_arrival(turn, step):
        other = lax.rem(h + owners - step, owners)
        return pltpu.make_async_remote_copy(
            src_ref=bs.at[turn, other],
            dst_ref=br.at[turn, other],
            send_sem=b_send.at[turn, step],
            recv_sem=b_recv.at[turn, step],
            device_id=(r, other),
            device_id_type=MESH,
        )

    def send_rims(turn):
        for copy, dirs in ((x_copy, X_DIRS), (y_copy, Y_DIRS)):
            for slot, direction in enumerate(dirs):
                there, device = target(direction)

                @pl.when(there)
                def _(copy=copy, slot=slot, device=device):
                    copy(turn, slot, device).start()

    def wait_rims(turn):
        for copy, dirs in ((x_copy, X_DIRS), (y_copy, Y_DIRS)):
            for slot, direction in enumerate(dirs):
                there, device = source(direction)

                @pl.when(there)
                def _(copy=copy, slot=slot, device=device):
                    copy(turn, slot, device).wait_recv()

    def wait_sends(turn):
        for copy, dirs in ((x_copy, X_DIRS), (y_copy, Y_DIRS)):
            for slot, direction in enumerate(dirs):
                there, device = target(direction)

                @pl.when(there)
                def _(copy=copy, slot=slot, device=device):
                    copy(turn, slot, device).wait_send()

        for step in range(1, owners):
            b_copy(turn, step).wait_send()

    def put_rims(turn, fields):
        to_next, to_before = pack_x(fields)
        xs[turn][0] = to_next
        xs[turn][1] = to_before
        tiles = pack_y(fields)
        ys[turn, : tiles.shape[0]] = tiles

    def take_rims(turn, count):
        rim_x = unpack_x(xr[turn][0], xr[turn][1])
        column = (iota((1, 8, 128), 2) & 7) < RIM
        before = jnp.where(column, yr[turn, 4], yr[turn, 5])
        beside = jnp.where(column, yr[turn, 2], yr[turn, 3])
        after = jnp.where(column, yr[turn, 0], yr[turn, 1])
        corner = jnp.where(iota((1, 8, 128), 1) < RIM, after, before)
        return rim_x, unpack_y(beside, count), unpack_y(corner, 3 * nz)


    cells = load(cells_ref)[0].astype(F32)
    wide = (slots, slots * FOOTPRINT_CELLS)
    own = (iota(wide, 1) // FOOTPRINT_CELLS) == iota(wide, 0)
    corner_cell = jnp.min(jnp.where(own, cells, 1e9), axis=1, keepdims=True)
    corner_x = jnp.floor(corner_cell * (1.0 / 128.0))
    corner_y = corner_cell - 128.0 * corner_x
    lane = iota((slots, 128), 1)
    along_y = lane.astype(F32) - corner_y
    window_y = ((along_y == 0.0) | (along_y == 1.0)).astype(F32).astype(BF16)
    along_x = (lane & 7).astype(F32) - corner_x
    part = lane & 31
    slot_row = iota((slots, 1), 0)
    loads[id(counts_ref)].wait()
    row_counts = counts_ref[0, pl.ds(h, 1), :].astype(F32)
    pairs = (slots, owners)
    live_count = jnp.sum(
        jnp.where(iota(pairs, 0) // capacity == iota(pairs, 1), row_counts, 0.0),
        axis=1,
        keepdims=True,
    )
    live = (slot_row % capacity).astype(F32) < live_count
    weight = jnp.where(
        live & ((along_x == 0.0) | (along_x == 1.0)) & (part < 24), 1.0 / FOOTPRINT_CELLS, 0.0
    )
    square = (slots, slots)
    arch = jnp.sum(
        jnp.where(iota(square, 0) == iota(square, 1), load(arch_ref).astype(F32), 0.0),
        axis=1,
        keepdims=True,
    )
    is_kind = [arch == float(a) for a in range(kinds)]
    couple = load(couple_ref)
    coupling = []
    for c in range(3):
        chosen = jnp.zeros((slots, freedoms), F32)
        for a in range(kinds):
            chosen = jnp.where(is_kind[a], couple[c, a : a + 1, :], chosen)
        coupling.append(chosen)

    def surface_motion(field):
        surface = field[:, 0]
        high = surface.astype(BF16).astype(F32)
        nothing = jnp.zeros((8, 128), F32)
        stacked = jnp.concatenate(
            [high.reshape(24, 128), nothing, (surface - high).reshape(24, 128), nothing]
            + [nothing] * 8,
            axis=0,
        ).astype(BF16)
        gathered = lax.dot_general(
            window_y, stacked, (((1,), (1,)), ((), ())), preferred_element_type=F32
        )
        return gathered * weight

    def base_shear(state):
        shear = [jnp.sum(coupling[c] * state, axis=1, keepdims=True) for c in range(3)]
        return jnp.where(part < 8, shear[0], jnp.where(part < 16, shear[1], shear[2]))

    def put_buildings(turn, field, state):
        both = jnp.where(lane < 64, surface_motion(field), base_shear(state))
        both = both.reshape(owners, capacity, 128)
        bs[turn] = both
        br[turn, h] = bs[turn, h]

    def send_buildings(turn):
        for step in range(owners // 2, 0, -1):
            b_copy(turn, step).start()
            if owners - step != step:
                b_copy(turn, owners - step).start()

    def take_buildings(turn):
        for step in range(1, owners):
            b_arrival(turn, step).wait_recv()
        both = br[turn].reshape(slots, 128)
        drive = jnp.zeros((slots, freedoms), F32)
        for c in range(3):
            mine = (lane < 64) & (part >= 8 * c) & (part < 8 * c + 8)
            base = jnp.sum(jnp.where(mine, both, 0.0), axis=1, keepdims=True)
            drive = drive + coupling[c] * base
        pull = both * weight
        high = pull.astype(BF16).astype(F32)
        pull = jnp.where((lane & 32) == 0, high, pull - high)
        spread = lax.dot_general(
            pull.T.astype(BF16), window_y, (((1,), (0,)), ((), ())), preferred_element_type=F32
        )
        force = (spread[64:88] + spread[96:120]).reshape(3, 8, 128)
        return drive, force

    def stiff_term(state):
        high, low = split(state)
        stacked = jnp.concatenate([high.astype(F32), low.astype(F32)], axis=0)
        twice = jnp.concatenate([arch, arch], axis=0)
        spread = jnp.concatenate(
            [jnp.where(twice == float(a), stacked, 0.0).astype(BF16) for a in range(kinds)],
            axis=1,
        )
        product = jnp.dot(spread, table[...], preferred_element_type=F32)
        product = product[:, :freedoms] + product[:, freedoms:]
        return product[:slots] + product[slots:]

    u, q = load(u_ref), load(q_ref)
    put_buildings(0, u, q)
    lam, mu = load(lam_ref) * (1.0 / 144.0), load(mu_ref) * (1.0 / 144.0)
    put_rims(0, jnp.concatenate([u.reshape(3 * nz, 8, 128), lam, mu], axis=0))
    pl.semaphore_wait(barrier, arrivals)
    send_buildings(0)
    send_rims(0)
    stiff_high, stiff_low = split(load(stiff_ref).reshape(kinds * freedoms, freedoms))
    table[:, :freedoms] = stiff_high
    table[:, freedoms:] = stiff_low
    stiff = stiff_term(q)
    u_old, q_old = load(u_prev_ref), load(q_prev_ref)
    gain = load(buoy_ref) * (TIME_STEP * TIME_STEP)
    count = 5 * nz
    lam_mu_x = lam_mu_y = None
    for turn in range(STEPS):
        wait_rims(turn)
        rim_x, rim_y, corner = take_rims(turn, count)
        if turn == 0:
            lam_mu_x, lam_mu_y = rim_x[3 * nz :], rim_y[3 * nz :]
        shape = (3, nz, 8, 128)
        total = divergence(
            u,
            rim_x[: 3 * nz].reshape(shape),
            rim_y[: 3 * nz].reshape(shape),
            corner.reshape(shape),
            lam,
            mu,
            lam_mu_x[:nz],
            lam_mu_x[nz:],
            lam_mu_y[:nz],
            lam_mu_y[nz:],
        )
        drive, force = take_buildings(turn)
        q, q_old = 2.0 * q - q_old + (TIME_STEP * TIME_STEP) * (drive - stiff), q
        total = jnp.concatenate([total[:, :1] + force[:, None], total[:, 1:]], axis=1)
        u, u_old = 2.0 * u - u_old + gain * total, u
        count = 3 * nz
        if turn + 1 < STEPS:
            put_buildings(turn + 1, u, q)
            send_buildings(turn + 1)
            put_rims(turn + 1, u.reshape(3 * nz, 8, 128))
            send_rims(turn + 1)
            u_before_ref[...] = u
            q_before_ref[...] = q
            stiff = stiff_term(q)
    u_last_ref[...] = u
    q_last_ref[...] = q
    for turn in range(STEPS):
        wait_sends(turn)


def shards(
    rows,
    owners,
    u_now,
    u_prev,
    lame_lambda,
    lame_mu,
    buoyancy,
    q_now,
    q_prev,
    archetype,
    stiffness,
    couple,
    counts,
    footprint,
):
    nz = lame_mu.shape[0]
    slots, freedoms = q_now.shape
    capacity = slots // owners
    kinds = stiffness.shape[0]
    pairs = (5 * nz) // 2, (3 * nz) // 2
    vmem = pl.BlockSpec(memory_space=pltpu.VMEM)
    hbm = pl.BlockSpec(memory_space=pltpu.HBM)
    dma = pltpu.SemaphoreType.DMA
    operands = (
        u_now,
        u_prev,
        lame_lambda,
        lame_mu,
        buoyancy,
        q_now,
        q_prev,
        archetype.reshape(1, slots),
        stiffness,
        couple.transpose(1, 0, 2),
        counts,
        footprint,
    )
    results = (
        jax.ShapeDtypeStruct(u_now.shape, F32),
        jax.ShapeDtypeStruct(u_now.shape, F32),
        jax.ShapeDtypeStruct(q_now.shape, F32),
        jax.ShapeDtypeStruct(q_now.shape, F32),
    )
    held = pl.pallas_call(
        functools.partial(kernel, rows, owners),
        out_shape=tuple(pltpu.VMEM(result.shape, result.dtype) for result in results),
        in_specs=[hbm] * len(operands),
        out_specs=(vmem,) * 4,
        scratch_shapes=[
            pltpu.VMEM((2, pairs[0], 8, 128), F32),
            pltpu.VMEM((2, pairs[1], 8, 128), F32),
            pltpu.VMEM((2, pairs[0], 8, 128), F32),
            pltpu.VMEM((2, pairs[1], 8, 128), F32),
            pltpu.VMEM((STEPS, 2, 8, 128), F32),
            pltpu.VMEM((STEPS, len(Y_DIRS), 2, 8, 128), F32),
            pltpu.VMEM((STEPS, owners, capacity, 128), F32),
            pltpu.VMEM((STEPS, owners, capacity, 128), F32),
            pltpu.VMEM((kinds * freedoms, 2 * freedoms), BF16),
        ]
        + [pltpu.VMEM(operand.shape, operand.dtype) for operand in operands]
        + [
            dma((len(operands),)),
            dma((STEPS, 2)),
            dma((STEPS, 2)),
            dma((STEPS, len(Y_DIRS))),
            dma((STEPS, len(Y_DIRS))),
            dma((STEPS, owners)),
            dma((STEPS, owners)),
        ],
        compiler_params=pltpu.CompilerParams(
            collective_id=0, has_side_effects=True, vmem_limit_bytes=60 * 1024 * 1024
        ),
    )(*operands)
    return pl.pallas_call(
        store,
        out_shape=results,
        in_specs=[vmem] * 4,
        out_specs=(hbm,) * 4,
        scratch_shapes=[dma((4,))],
        compiler_params=pltpu.CompilerParams(vmem_limit_bytes=1024 * 1024),
    )(*held)


def store(*refs):
    copies = [
        pltpu.make_async_copy(refs[k], refs[4 + k], refs[8].at[k]) for k in range(4)
    ]
    for copy in copies:
        copy.start()
    for copy in copies:
        copy.wait()


def solution(mesh):
    return jax.shard_map(
        functools.partial(shards, mesh.shape["gx"], mesh.shape["gy"]),
        mesh=mesh,
        in_specs=(
            P(None, None, "gx", "gy"),
            P(None, None, "gx", "gy"),
            P(None, "gx", "gy"),
            P(None, "gx", "gy"),
            P(None, "gx", "gy"),
            P(("gx", "gy"), None),
            P(("gx", "gy"), None),
            P(("gx", "gy")),
            P(),
            P(),
            P("gx", None, None),
            P("gx", "gy", None),
        ),
        out_specs=(
            P(None, None, "gx", "gy"),
            P(None, None, "gx", "gy"),
            P(("gx", "gy"), None),
            P(("gx", "gy"), None),
        ),
        check_vma=False,
    )
```

profile of v0, /device:TPU:1, one launch (start us, length us, event | category | flops | bytes accessed | tf_op | source)
XLA Modules:
  0.0 15.1 jit_solution(1601525873746670202)
XLA Ops:
  0.6 13.7 %shard_map.147 = (f32[3,6,8,128]{3,2,1,0:T(8,128)S(1)}, f32[3,6,8,128]{3,2,1,0:T(8,128)S(1)}, f32[64,128]{1,0:T(8,128)S(1)}, f32[64,128]{1,0:T(8,128)S(1)}) custom-call(f32[3,6,8,128]{3,2,1,0:T(8,128)} %u_hbm.1, f32[3,6,8,128]{3,2,1,0:T(8,128)} %u_prev_hbm.1, f32[6,8,128]{2,1,0:T(8,128)} %lam_hbm.1, f32[6,8,128]{2,1,0:T(8,128)} %mu_hbm.1, ...), custom_call_target="tpu_custom_call" | custom-call | tf_op jit(solution)/shard_map/pallas_call | solution.py:534
  14.4 0.7 %shard_map.148 = (f32[3,6,8,128]{3,2,1,0:T(8,128)}, f32[3,6,8,128]{3,2,1,0:T(8,128)}, f32[64,128]{1,0:T(8,128)}, f32[64,128]{1,0:T(8,128)}) custom-call(f32[3,6,8,128]{3,2,1,0:T(8,128)S(1)} %get-tuple-element.8.refs_0_, f32[3,6,8,128]{3,2,1,0:T(8,128)S(1)} %get-tuple-element.9.refs_1_, f32[64,128]{1,0:T(8,128)S(1)} %get-tuple-element.10.refs_2_, ...), custom_call_target="tpu_custom_call" | custom-call | tf_op jit(solution)/shard_map/pallas_call | solution.py:564
where the time goes:
time: 15.3 us; the launch traced here: 15.1 us
  Pallas kernels  14.4 us (94%)
  between operations  0.64 us (4%)
    pallas_call x1, Pallas kernels, shards(): pl.pallas_call(functools.partial(kernel, rows, owners), out_shape=tuple((...  13.7 us
    pallas_call x1, Pallas kernels, shards(): pl.pallas_call(store, out_shape=results, in_specs=[vmem] * 4, out_specs=(...  0.71 us

commit v1 on v0

--- a/solution.py
+++ b/solution.py
@@ -149,8 +149,12 @@
     xr1,
     ys,
     yr,
-    bs,
-    br,
+    a_out,
+    a_in,
+    w_out,
+    w_in,
+    p_out,
+    p_in,
     table,
     u_ref,
     u_prev_ref,
@@ -171,6 +175,7 @@
     y_recv,
     b_send,
     b_recv,
+    entered,
 ):
     r, h = lax.axis_index("gx"), lax.axis_index("gy")
     nz = lam_ref.shape[0]
@@ -178,6 +183,7 @@
     capacity = slots // owners
     kinds = stiff_ref.shape[0]
     freedoms = q_ref.shape[1]
+    dt2 = TIME_STEP * TIME_STEP
     xs, xr = (xs0, xs1), (xr0, xr1)
 
     def target(direction):
@@ -192,13 +198,32 @@
     def source(direction):
         return target((-direction[0], -direction[1]))
 
+    loads = {}
+
+    def start_loads(pairs):
+        for source_ref, ref in pairs:
+            copy = pltpu.make_async_copy(source_ref, ref, loaded.at[len(loads)])
+            copy.start()
+            loads[id(ref)] = copy
+
+    start_loads(
+        (
+            (q_hbm, q_ref),
+            (couple_hbm, couple_ref),
+            (arch_hbm, arch_ref),
+            (u_hbm, u_ref),
+        )
+    )
     peers = X_DIRS + tuple(d for d in Y_DIRS if d[0])
 
     barrier = pltpu.get_barrier_semaphore()
-    arrivals = jnp.int32(owners - 1)
+    arrivals = h + (h + 1 < owners).astype(jnp.int32)
     for step in range(1, owners):
         other = lax.rem(h + step, owners)
-        pl.semaphore_signal(barrier, inc=1, device_id=(r, other), device_id_type=MESH)
+
+        @pl.when((h + step < owners) | (step == owners - 1))
+        def _(other=other):
+            pl.semaphore_signal(barrier, inc=1, device_id=(r, other), device_id_type=MESH)
 
     for direction in peers:
         there, device = target(direction)
@@ -208,24 +233,18 @@
         def _(device=device):
             pl.semaphore_signal(barrier, inc=1, device_id=device, device_id_type=MESH)
 
-    loads = {}
-    for source_ref, ref in (
-        (cells_hbm, cells_ref),
-        (counts_hbm, counts_ref),
-        (arch_hbm, arch_ref),
-        (couple_hbm, couple_ref),
-        (u_hbm, u_ref),
-        (q_hbm, q_ref),
-        (lam_hbm, lam_ref),
-        (mu_hbm, mu_ref),
-        (stiff_hbm, stiff_ref),
-        (q_prev_hbm, q_prev_ref),
-        (u_prev_hbm, u_prev_ref),
-        (buoy_hbm, buoy_ref),
-    ):
-        copy = pltpu.make_async_copy(source_ref, ref, loaded.at[len(loads)])
-        copy.start()
-        loads[id(ref)] = copy
+    start_loads(
+        (
+            (lam_hbm, lam_ref),
+            (mu_hbm, mu_ref),
+            (stiff_hbm, stiff_ref),
+            (q_prev_hbm, q_prev_ref),
+            (cells_hbm, cells_ref),
+            (counts_hbm, counts_ref),
+            (buoy_hbm, buoy_ref),
+            (u_prev_hbm, u_prev_ref),
+        )
+    )
 
     for slot, direction in enumerate(X_DIRS):
         there, _ = source(direction)
@@ -267,24 +286,28 @@
             device_id_type=MESH,
         )
 
-    def b_copy(turn, step):
+    messages = ((a_out, a_in), (w_out, w_in), (p_out, p_in))
+
+    def b_copy(which, step):
         other = lax.rem(h + step, owners)
+        out, into = messages[which]
         return pltpu.make_async_remote_copy(
-            src_ref=bs.at[turn, other],
-            dst_ref=br.at[turn, h],
-            send_sem=b_send.at[turn, step],
-            recv_sem=b_recv.at[turn, step],
+            src_ref=out if which == 0 else out.at[other],
+            dst_ref=into.at[h],
+            send_sem=b_send.at[which, step],
+            recv_sem=b_recv.at[which, step],
             device_id=(r, other),
             device_id_type=MESH,
         )
 
-    def b_arrival(turn, step):
+    def b_arrival(which, step):
         other = lax.rem(h + owners - step, owners)
+        out, into = messages[which]
         return pltpu.make_async_remote_copy(
-            src_ref=bs.at[turn, other],
-            dst_ref=br.at[turn, other],
-            send_sem=b_send.at[turn, step],
-            recv_sem=b_recv.at[turn, step],
+            src_ref=out if which == 0 else out.at[other],
+            dst_ref=into.at[other],
+            send_sem=b_send.at[which, step],
+            recv_sem=b_recv.at[which, step],
             device_id=(r, other),
             device_id_type=MESH,
         )
@@ -307,17 +330,19 @@
                 def _(copy=copy, slot=slot, device=device):
                     copy(turn, slot, device).wait_recv()
 
-    def wait_sends(turn):
-        for copy, dirs in ((x_copy, X_DIRS), (y_copy, Y_DIRS)):
-            for slot, direction in enumerate(dirs):
-                there, device = target(direction)
-
-                @pl.when(there)
-                def _(copy=copy, slot=slot, device=device):
-                    copy(turn, slot, device).wait_send()
-
-        for step in range(1, owners):
-            b_copy(turn, step).wait_send()
+    def wait_sends():
+        for turn in range(STEPS):
+            for copy, dirs in ((x_copy, X_DIRS), (y_copy, Y_DIRS)):
+                for slot, direction in enumerate(dirs):
+                    there, device = target(direction)
+
+                    @pl.when(there)
+                    def _(copy=copy, slot=slot, device=device, turn=turn):
+                        copy(turn, slot, device).wait_send()
+
+        for which in range(len(messages)):
+            for step in range(1, owners):
+                b_copy(which, step).wait_send()
 
     def put_rims(turn, fields):
         to_next, to_before = pack_x(fields)
@@ -335,6 +360,73 @@
         corner = jnp.where(iota((1, 8, 128), 1) < RIM, after, before)
         return rim_x, unpack_y(beside, count), unpack_y(corner, 3 * nz)
 
+    def send_buildings(which):
+        for step in range(owners // 2, 0, -1):
+            b_copy(which, step).start()
+            if owners - step != step:
+                b_copy(which, owners - step).start()
+
+    def take_buildings(which):
+        for step in range(1, owners):
+            b_arrival(which, step).wait_recv()
+        into = messages[which][1]
+        return into[...].reshape(slots, into.shape[2])
+
+    lane = iota((slots, 128), 1)
+    part = lane & 31
+    slot_row = iota((slots, 1), 0)
+    square = (slots, slots)
+
+    couple = load(couple_ref)
+    arch = jnp.sum(
+        jnp.where(iota(square, 0) == iota(square, 1), load(arch_ref).astype(F32), 0.0),
+        axis=1,
+        keepdims=True,
+    )
+    is_kind = [arch == float(a) for a in range(kinds)]
+    coupling = []
+    for c in range(3):
+        chosen = jnp.zeros((slots, freedoms), F32)
+        for a in range(kinds):
+            chosen = jnp.where(is_kind[a], couple[c, a : a + 1, :], chosen)
+        coupling.append(chosen)
+
+    def couple_sum(c, state):
+        return jnp.sum(coupling[c] * state, axis=1, keepdims=True)
+
+    q = load(q_ref)
+    shear = [couple_sum(c, q) for c in range(3)]
+    shear = jnp.where(part < 8, shear[0], jnp.where(part < 16, shear[1], shear[2]))
+    shear = shear.reshape(owners, capacity, 128)
+    group = iota((capacity, 128), 1) // 32
+    for t in range(a_out.shape[1] // 128):
+        tile = shear[4 * t]
+        for k in range(1, 4):
+            if 4 * t + k < owners:
+                tile = jnp.where(group == k, shear[4 * t + k], tile)
+        a_out[:, 128 * t : 128 * (t + 1)] = tile
+    a_in[h] = a_out[...]
+
+    u = load(u_ref)
+    lam, mu = load(lam_ref) * (1.0 / 144.0), load(mu_ref) * (1.0 / 144.0)
+    put_rims(0, jnp.concatenate([u.reshape(3 * nz, 8, 128), lam, mu], axis=0))
+    pl.semaphore_wait(barrier, arrivals)
+    for step in range(1, owners - 1):
+        other = lax.rem(h + step, owners)
+
+        @pl.when(h + step >= owners)
+        def _(step=step, other=other):
+            pl.semaphore_signal(
+                entered.at[owners - step], inc=1, device_id=(r, other), device_id_type=MESH
+            )
+
+    for step in range(1, owners):
+
+        @pl.when((h + step >= owners) | (step == 1))
+        def _(step=step):
+            b_copy(0, step).start()
+
+    send_rims(0)
 
     cells = load(cells_ref)[0].astype(F32)
     wide = (slots, slots * FOOTPRINT_CELLS)
@@ -342,12 +434,10 @@
     corner_cell = jnp.min(jnp.where(own, cells, 1e9), axis=1, keepdims=True)
     corner_x = jnp.floor(corner_cell * (1.0 / 128.0))
     corner_y = corner_cell - 128.0 * corner_x
-    lane = iota((slots, 128), 1)
     along_y = lane.astype(F32) - corner_y
-    window_y = ((along_y == 0.0) | (along_y == 1.0)).astype(F32).astype(BF16)
+    in_y = ((along_y == 0.0) | (along_y == 1.0)).astype(F32)
+    window_y = in_y.astype(BF16)
     along_x = (lane & 7).astype(F32) - corner_x
-    part = lane & 31
-    slot_row = iota((slots, 1), 0)
     loads[id(counts_ref)].wait()
     row_counts = counts_ref[0, pl.ds(h, 1), :].astype(F32)
     pairs = (slots, owners)
@@ -360,20 +450,11 @@
     weight = jnp.where(
         live & ((along_x == 0.0) | (along_x == 1.0)) & (part < 24), 1.0 / FOOTPRINT_CELLS, 0.0
     )
-    square = (slots, slots)
-    arch = jnp.sum(
-        jnp.where(iota(square, 0) == iota(square, 1), load(arch_ref).astype(F32), 0.0),
-        axis=1,
-        keepdims=True,
-    )
-    is_kind = [arch == float(a) for a in range(kinds)]
-    couple = load(couple_ref)
-    coupling = []
-    for c in range(3):
-        chosen = jnp.zeros((slots, freedoms), F32)
-        for a in range(kinds):
-            chosen = jnp.where(is_kind[a], couple[c, a : a + 1, :], chosen)
-        coupling.append(chosen)
+    base_weight = jnp.where(lane < 64, weight, 0.0)
+    mine = [(lane < 64) & (part >= 8 * c) & (part < 8 * c + 8) for c in range(3)]
+
+    def group_sum(c, value):
+        return jnp.sum(jnp.where(mine[c], value, 0.0), axis=1, keepdims=True)
 
     def surface_motion(field):
         surface = field[:, 0]
@@ -387,41 +468,21 @@
         gathered = lax.dot_general(
             window_y, stacked, (((1,), (1,)), ((), ())), preferred_element_type=F32
         )
-        return gathered * weight
-
-    def base_shear(state):
-        shear = [jnp.sum(coupling[c] * state, axis=1, keepdims=True) for c in range(3)]
-        return jnp.where(part < 8, shear[0], jnp.where(part < 16, shear[1], shear[2]))
-
-    def put_buildings(turn, field, state):
-        both = jnp.where(lane < 64, surface_motion(field), base_shear(state))
-        both = both.reshape(owners, capacity, 128)
-        bs[turn] = both
-        br[turn, h] = bs[turn, h]
-
-    def send_buildings(turn):
-        for step in range(owners // 2, 0, -1):
-            b_copy(turn, step).start()
-            if owners - step != step:
-                b_copy(turn, owners - step).start()
-
-    def take_buildings(turn):
-        for step in range(1, owners):
-            b_arrival(turn, step).wait_recv()
-        both = br[turn].reshape(slots, 128)
-        drive = jnp.zeros((slots, freedoms), F32)
-        for c in range(3):
-            mine = (lane < 64) & (part >= 8 * c) & (part < 8 * c + 8)
-            base = jnp.sum(jnp.where(mine, both, 0.0), axis=1, keepdims=True)
-            drive = drive + coupling[c] * base
-        pull = both * weight
+        return gathered * base_weight
+
+    def surface_force(pull):
         high = pull.astype(BF16).astype(F32)
         pull = jnp.where((lane & 32) == 0, high, pull - high)
         spread = lax.dot_general(
             pull.T.astype(BF16), window_y, (((1,), (0,)), ((), ())), preferred_element_type=F32
         )
-        force = (spread[64:88] + spread[96:120]).reshape(3, 8, 128)
-        return drive, force
+        return (spread[0:24] + spread[32:56]).reshape(3, 8, 128)
+
+    def drive_of(base):
+        drive = coupling[0] * base[0]
+        for c in range(1, 3):
+            drive = drive + coupling[c] * base[c]
+        return drive
 
     def stiff_term(state):
         high, low = split(state)
@@ -435,29 +496,64 @@
         product = product[:, :freedoms] + product[:, freedoms:]
         return product[:slots] + product[slots:]
 
-    u, q = load(u_ref), load(q_ref)
-    put_buildings(0, u, q)
-    lam, mu = load(lam_ref) * (1.0 / 144.0), load(mu_ref) * (1.0 / 144.0)
-    put_rims(0, jnp.concatenate([u.reshape(3 * nz, 8, 128), lam, mu], axis=0))
-    pl.semaphore_wait(barrier, arrivals)
-    send_buildings(0)
-    send_rims(0)
+    base = surface_motion(u)
+    home_base = [group_sum(c, base) for c in range(3)]
+
+    gain = load(buoy_ref) * dt2
+    overlap_left, overlap_right = [], []
+    for x in range(8):
+        there = live & ((corner_x == float(x)) | (corner_x == float(x - 1)))
+        window = jnp.where(there, in_y, 0.0)
+        overlap_right.append(window)
+        overlap_left.append(window * (gain[0, x : x + 1, :] * (1.0 / FOOTPRINT_CELLS**2)))
+    left_high, left_low = split(jnp.concatenate(overlap_left, axis=1))
+    right = jnp.concatenate(overlap_right, axis=1)
+    width = w_out.shape[2]
+    blank = [jnp.zeros((64, right.shape[1]), F32)]
+    spare = width - 64 - slots
+    after = [jnp.zeros((spare, right.shape[1]), F32)] if spare else []
+    right = jnp.concatenate(blank + [right] + after, axis=0).astype(BF16)
+    nt = (((1,), (1,)), ((), ()))
+    overlap = lax.dot_general(left_high, right, nt, preferred_element_type=F32)
+    overlap = overlap + lax.dot_general(left_low, right, nt, preferred_element_type=F32)
+
     stiff_high, stiff_low = split(load(stiff_ref).reshape(kinds * freedoms, freedoms))
     table[:, :freedoms] = stiff_high
     table[:, freedoms:] = stiff_low
-    stiff = stiff_term(q)
-    u_old, q_old = load(u_prev_ref), load(q_prev_ref)
-    gain = load(buoy_ref) * (TIME_STEP * TIME_STEP)
-    count = 5 * nz
-    lam_mu_x = lam_mu_y = None
-    for turn in range(STEPS):
-        wait_rims(turn)
+    coasting = 2.0 * q - load(q_prev_ref) - dt2 * stiff_term(q)
+    fields = base
+    columns = [couple_sum(c, coasting) for c in range(3)]
+    pairs_of = ((0, 0), (0, 1), (0, 2), (1, 1), (1, 2), (2, 2))
+    columns += [dt2 * couple_sum(c, coupling[d]) for c, d in pairs_of]
+    places = (24, 25, 26, 27, 28, 29, 30, 31, 56)
+    for place, column in zip(places, columns):
+        fields = jnp.where(lane == place, column, fields)
+    first = jnp.where(lane < 64, fields, overlap[:, :128])
+    if width > 128:
+        first = jnp.concatenate([first, overlap[:, 128:]], axis=1)
+    w_out[...] = first.reshape(owners, capacity, width)
+    w_in[h] = w_out[h]
+    for step in range(2, owners):
+
+        @pl.when(h + step < owners)
+        def _(step=step):
+            pl.semaphore_wait(entered.at[step], 1)
+            b_copy(0, step).start()
+
+    send_buildings(1)
+
+    u_old = load(u_prev_ref)
+
+    shape = (3, nz, 8, 128)
+
+    def push(turn, field, lam_mu):
+        count = (5 if turn == 0 else 3) * nz
         rim_x, rim_y, corner = take_rims(turn, count)
         if turn == 0:
-            lam_mu_x, lam_mu_y = rim_x[3 * nz :], rim_y[3 * nz :]
-        shape = (3, nz, 8, 128)
+            lam_mu = rim_x[3 * nz :], rim_y[3 * nz :]
+        lam_mu_x, lam_mu_y = lam_mu
         total = divergence(
-            u,
+            field,
             rim_x[: 3 * nz].reshape(shape),
             rim_y[: 3 * nz].reshape(shape),
             corner.reshape(shape),
@@ -468,23 +564,74 @@
             lam_mu_y[:nz],
             lam_mu_y[nz:],
         )
-        drive, force = take_buildings(turn)
-        q, q_old = 2.0 * q - q_old + (TIME_STEP * TIME_STEP) * (drive - stiff), q
-        total = jnp.concatenate([total[:, :1] + force[:, None], total[:, 1:]], axis=1)
-        u, u_old = 2.0 * u - u_old + gain * total, u
-        count = 3 * nz
-        if turn + 1 < STEPS:
-            put_buildings(turn + 1, u, q)
-            send_buildings(turn + 1)
-            put_rims(turn + 1, u.reshape(3 * nz, 8, 128))
-            send_rims(turn + 1)
-            u_before_ref[...] = u
-            q_before_ref[...] = q
-            stiff = stiff_term(q)
-    u_last_ref[...] = u
-    q_last_ref[...] = q
-    for turn in range(STEPS):
-        wait_sends(turn)
+        return total, lam_mu
+
+    def on_surface(field, force):
+        return jnp.concatenate([field[:, :1] + (gain[0] * force)[:, None], field[:, 1:]], axis=1)
+
+    wait_rims(0)
+    total, lam_mu = push(0, u, None)
+    free = 2.0 * u - u_old + gain * total
+    p_out[...] = surface_motion(free).reshape(owners, capacity, 128)
+    p_in[h] = p_out[h]
+    send_buildings(2)
+
+    shears = take_buildings(0)
+    pull = jnp.zeros((slots, 128), F32)
+    for t in range(a_out.shape[1] // 128):
+        here = (lane // 32 + 4 * t) == h
+        pull = pull + jnp.where(here, shears[:, 128 * t : 128 * (t + 1)], 0.0)
+    pull = pull + pltpu.roll(pull, 64, 1)
+    pull = pull + pltpu.roll(pull, 32, 1)
+    u_new = on_surface(free, surface_force(pull * weight))
+    u, u_old = u_new, u
+    put_rims(1, u.reshape(3 * nz, 8, 128))
+    send_rims(1)
+    u_before_ref[...] = u
+
+    words = take_buildings(1)
+    low_words = words[:, :128]
+    drive = drive_of([group_sum(c, low_words) for c in range(3)])
+    q, q_old = coasting + dt2 * drive, q
+    q_before_ref[...] = q
+    stiff = stiff_term(q)
+
+    gram = {}
+    for place, pair in zip(places[3:], pairs_of):
+        gram[pair] = gram[pair[::-1]] = low_words[:, place : place + 1]
+    later = []
+    for c in range(3):
+        value = low_words[:, 24 + c : 25 + c]
+        for d in range(3):
+            value = value + gram[c, d] * home_base[d]
+        later.append(value)
+    later = jnp.where(part < 8, later[0], jnp.where(part < 16, later[1], later[2]))
+    force = surface_force(later * weight)
+
+    left_high, left_low = split(words)
+    blank = [jnp.zeros((64, shears.shape[1]), F32)]
+    after = [jnp.zeros((spare, shears.shape[1]), F32)] if spare else []
+    right = jnp.concatenate(blank + [shears] + after, axis=0)
+    right_high, right_low = split(right)
+    moved = jnp.dot(left_high, right_high, preferred_element_type=F32)
+    moved = moved + jnp.dot(left_low, right_high, preferred_element_type=F32)
+    moved = moved + jnp.dot(left_high, right_low, preferred_element_type=F32)
+    moved_lane = iota(moved.shape, 1)
+    moved_row = iota(moved.shape, 0) // capacity * 32
+    moved = [
+        jnp.sum(jnp.where(moved_lane == moved_row + 8 * c, moved, 0.0), axis=1, keepdims=True)
+        for c in range(3)
+    ]
+    q_free = 2.0 * q - q_old + dt2 * (drive_of(moved) - stiff)
+    u_free = on_surface(2.0 * u - u_old, force)
+
+    wait_rims(1)
+    total, _ = push(1, u, lam_mu)
+    u_last_ref[...] = u_free + gain * total
+
+    motion = take_buildings(2)
+    q_last_ref[...] = q_free + dt2 * drive_of([group_sum(c, motion) for c in range(3)])
+    wait_sends()
 
 
 def shards(
@@ -508,6 +655,8 @@
     capacity = slots // owners
     kinds = stiffness.shape[0]
     pairs = (5 * nz) // 2, (3 * nz) // 2
+    a_width = -(-32 * owners // 128) * 128
+    w_width = -(-(64 + slots) // 128) * 128
     vmem = pl.BlockSpec(memory_space=pltpu.VMEM)
     hbm = pl.BlockSpec(memory_space=pltpu.HBM)
     dma = pltpu.SemaphoreType.DMA
@@ -543,8 +692,12 @@
             pltpu.VMEM((2, pairs[1], 8, 128), F32),
             pltpu.VMEM((STEPS, 2, 8, 128), F32),
             pltpu.VMEM((STEPS, len(Y_DIRS), 2, 8, 128), F32),
-            pltpu.VMEM((STEPS, owners, capacity, 128), F32),
-            pltpu.VMEM((STEPS, owners, capacity, 128), F32),
+            pltpu.VMEM((capacity, a_width), F32),
+            pltpu.VMEM((owners, capacity, a_width), F32),
+            pltpu.VMEM((owners, capacity, w_width), F32),
+            pltpu.VMEM((owners, capacity, w_width), F32),
+            pltpu.VMEM((owners, capacity, 128), F32),
+            pltpu.VMEM((owners, capacity, 128), F32),
             pltpu.VMEM((kinds * freedoms, 2 * freedoms), BF16),
         ]
         + [pltpu.VMEM(operand.shape, operand.dtype) for operand in operands]
@@ -554,8 +707,9 @@
             dma((STEPS, 2)),
             dma((STEPS, len(Y_DIRS))),
             dma((STEPS, len(Y_DIRS))),
-            dma((STEPS, owners)),
-            dma((STEPS, owners)),
+            dma((3, owners)),
+            dma((3, owners)),
+            pltpu.SemaphoreType.REGULAR((owners,)),
         ],
         compiler_params=pltpu.CompilerParams(
             collective_id=0, has_side_effects=True, vmem_limit_bytes=60 * 1024 * 1024

time: 15.3 us -> 14.7 us (0.961)
  the two profiles are of different devices: /device:TPU:1 before, /device:TPU:3 now
where the time goes in v1:
time: 14.7 us; the launch traced here: 14.5 us
  Pallas kernels  13.9 us (95%)
  between operations  0.64 us (4%)
    pallas_call x1, Pallas kernels, shards(): pl.pallas_call(functools.partial(kernel, rows, owners), out_shape=tuple((...  13.2 us
    pallas_call x1, Pallas kernels, shards(): pl.pallas_call(store, out_shape=results, in_specs=[vmem] * 4, out_specs=(...  0.71 us

profile of v1, /device:TPU:3, one launch (start us, length us, event | category | flops | bytes accessed | tf_op | source)
XLA Modules:
  0.0 14.5 jit_solution(2345448909182430445)
XLA Ops:
  0.6 13.2 %shard_map.147 = (f32[3,6,8,128]{3,2,1,0:T(8,128)S(1)}, f32[3,6,8,128]{3,2,1,0:T(8,128)S(1)}, f32[64,128]{1,0:T(8,128)S(1)}, f32[64,128]{1,0:T(8,128)S(1)}) custom-call(f32[3,6,8,128]{3,2,1,0:T(8,128)} %u_hbm.1, f32[3,6,8,128]{3,2,1,0:T(8,128)} %u_prev_hbm.1, f32[6,8,128]{2,1,0:T(8,128)} %lam_hbm.1, f32[6,8,128]{2,1,0:T(8,128)} %mu_hbm.1, ...), custom_call_target="tpu_custom_call" | custom-call | tf_op jit(solution)/shard_map/pallas_call | solution.py:683
  13.8 0.7 %shard_map.148 = (f32[3,6,8,128]{3,2,1,0:T(8,128)}, f32[3,6,8,128]{3,2,1,0:T(8,128)}, f32[64,128]{1,0:T(8,128)}, f32[64,128]{1,0:T(8,128)}) custom-call(f32[3,6,8,128]{3,2,1,0:T(8,128)S(1)} %get-tuple-element.8.refs_0_, f32[3,6,8,128]{3,2,1,0:T(8,128)S(1)} %get-tuple-element.9.refs_1_, f32[64,128]{1,0:T(8,128)S(1)} %get-tuple-element.10.refs_2_, ...), custom_call_target="tpu_custom_call" | custom-call | tf_op jit(solution)/shard_map/pallas_call | solution.py:718

commit v2 on v1

--- a/solution.py
+++ b/solution.py
@@ -45,23 +45,22 @@
 
 
 def pack_y(fields):
-    count = fields.shape[0]
     lane = iota((8, 128), 1)
-    tiles = []
-    for start in range(0, count, 16):
-        tile = jnp.zeros((8, 128), F32)
-        for k in range(start, min(start + 16, count)):
-            place = 8 * (k - start)
-            moved = pltpu.roll(fields[k], (place + RIM) % 128, 1)
-            tile = jnp.where((lane >= place) & (lane < place + 8), moved, tile)
-        tiles.append(tile)
-    return jnp.stack(tiles)
-
-
-def unpack_y(tiles, count):
+    ahead, behind = jnp.zeros((8, 128), F32), jnp.zeros((8, 128), F32)
+    for k in range(fields.shape[0]):
+        place = RIM * k
+        moved = pltpu.roll(fields[k], (place + RIM) % 128, 1)
+        ahead = jnp.where((lane >= place) & (lane < place + RIM), moved, ahead)
+        behind = jnp.where((lane >= place + RIM) & (lane < place + 2 * RIM), moved, behind)
+    return ahead, behind
+
+
+def unpack_y(ahead, behind, count):
+    odd = (iota((8, 128), 1) & RIM) != 0
+    tiles = jnp.where(odd, behind, ahead), jnp.where(odd, ahead, behind)
     slabs = []
     for k in range(count):
-        slabs.append(pltpu.roll(tiles[k // 16], (124 - 8 * (k % 16)) % 128, 1))
+        slabs.append(pltpu.roll(tiles[k % 2], (124 - RIM * k) % 128, 1))
     return jnp.stack(slabs)
 
 
@@ -149,6 +148,7 @@
     xr1,
     ys,
     yr,
+    cr,
     a_out,
     a_in,
     w_out,
@@ -246,6 +246,14 @@
         )
     )
 
+    def half(ref, dx):
+        return ref if dx == 0 else ref.at[pl.ds(RIM if dx > 0 else 0, RIM)]
+
+    def y_place(turn, direction):
+        dx, dy = direction
+        k = 0 if dy > 0 else 1
+        return half((cr if dx else yr).at[turn, k], dx)
+
     for slot, direction in enumerate(X_DIRS):
         there, _ = source(direction)
 
@@ -258,9 +266,10 @@
         there, _ = source(direction)
 
         @pl.when(jnp.logical_not(there))
-        def _(slot=slot):
+        def _(direction=direction):
             for turn in range(STEPS):
-                yr[turn, slot] = jnp.zeros(yr.shape[2:], F32)
+                ref = y_place(turn, direction)
+                ref[...] = jnp.zeros(ref.shape, F32)
 
     def load(ref):
         loads[id(ref)].wait()
@@ -278,8 +287,8 @@
 
     def y_copy(turn, slot, device):
         return pltpu.make_async_remote_copy(
-            src_ref=ys.at[turn],
-            dst_ref=yr.at[turn, slot],
+            src_ref=half(ys.at[turn, 0 if Y_DIRS[slot][1] > 0 else 1], Y_DIRS[slot][0]),
+            dst_ref=y_place(turn, Y_DIRS[slot]),
             send_sem=y_send.at[turn, slot],
             recv_sem=y_recv.at[turn, slot],
             device_id=device,
@@ -348,17 +357,12 @@
         to_next, to_before = pack_x(fields)
         xs[turn][0] = to_next
         xs[turn][1] = to_before
-        tiles = pack_y(fields)
-        ys[turn, : tiles.shape[0]] = tiles
+        ys[turn, 0], ys[turn, 1] = pack_y(fields)
 
     def take_rims(turn, count):
         rim_x = unpack_x(xr[turn][0], xr[turn][1])
-        column = (iota((1, 8, 128), 2) & 7) < RIM
-        before = jnp.where(column, yr[turn, 4], yr[turn, 5])
-        beside = jnp.where(column, yr[turn, 2], yr[turn, 3])
-        after = jnp.where(column, yr[turn, 0], yr[turn, 1])
-        corner = jnp.where(iota((1, 8, 128), 1) < RIM, after, before)
-        return rim_x, unpack_y(beside, count), unpack_y(corner, 3 * nz)
+        rim_y = unpack_y(yr[turn, 0], yr[turn, 1], count)
+        return rim_x, rim_y, unpack_y(cr[turn, 0], cr[turn, 1], 3 * nz)
 
     def send_buildings(which):
         for step in range(owners // 2, 0, -1):
@@ -369,8 +373,10 @@
     def take_buildings(which):
         for step in range(1, owners):
             b_arrival(which, step).wait_recv()
-        into = messages[which][1]
-        return into[...].reshape(slots, into.shape[2])
+        into = messages[which][1][...]
+        if into.shape[1] < capacity:
+            into = jnp.concatenate([into, pltpu.roll(into, into.shape[2] // 2, 2)], axis=1)
+        return into.reshape(slots, into.shape[2])
 
     lane = iota((slots, 128), 1)
     part = lane & 31
@@ -396,14 +402,17 @@
 
     q = load(q_ref)
     shear = [couple_sum(c, q) for c in range(3)]
-    shear = jnp.where(part < 8, shear[0], jnp.where(part < 16, shear[1], shear[2]))
-    shear = shear.reshape(owners, capacity, 128)
-    group = iota((capacity, 128), 1) // 32
-    for t in range(a_out.shape[1] // 128):
-        tile = shear[4 * t]
-        for k in range(1, 4):
-            if 4 * t + k < owners:
-                tile = jnp.where(group == k, shear[4 * t + k], tile)
+    word = lane & 15
+    shear = jnp.where(word < 4, shear[0], jnp.where(word < 8, shear[1], shear[2]))
+    shear = shear.reshape(owners, 2, 8, 128)
+    group = iota((8, 128), 1) // 16
+    a_width = a_out.shape[1]
+    for t in range(a_width // 128):
+        tile = jnp.zeros((8, 128), F32)
+        for k in range(8):
+            which, home = divmod(8 * t + k, a_width // 32)
+            if home < owners:
+                tile = jnp.where(group == k, shear[home, which], tile)
         a_out[:, 128 * t : 128 * (t + 1)] = tile
     a_in[h] = a_out[...]
 
@@ -470,9 +479,11 @@
         )
         return gathered * base_weight
 
+    def halves(pull):
+        high = pull.astype(BF16).astype(F32)
+        return jnp.where((lane & 32) == 0, high, pull - high)
+
     def surface_force(pull):
-        high = pull.astype(BF16).astype(F32)
-        pull = jnp.where((lane & 32) == 0, high, pull - high)
         spread = lax.dot_general(
             pull.T.astype(BF16), window_y, (((1,), (0,)), ((), ())), preferred_element_type=F32
         )
@@ -569,20 +580,27 @@
     def on_surface(field, force):
         return jnp.concatenate([field[:, :1] + (gain[0] * force)[:, None], field[:, 1:]], axis=1)
 
+    picked = (2 * a_width, 128)
+    place, column = iota(picked, 0), iota(picked, 1)
+    word = 16 * h + 4 * ((column & 31) // 8)
+    word = jnp.where(column < 32, word, word + a_width)
+    chosen = ((place == word) & (column < 64) & ((column & 31) < 24)).astype(F32).astype(BF16)
+
     wait_rims(0)
     total, lam_mu = push(0, u, None)
     free = 2.0 * u - u_old + gain * total
-    p_out[...] = surface_motion(free).reshape(owners, capacity, 128)
+    motion = surface_motion(free).reshape(owners, 2, 8, 128)
+    p_out[...] = jnp.where(
+        iota((owners, 8, 128), 2) < 64, motion[:, 0], pltpu.roll(motion[:, 1], 64, 2)
+    )
     p_in[h] = p_out[h]
     send_buildings(2)
 
     shears = take_buildings(0)
-    pull = jnp.zeros((slots, 128), F32)
-    for t in range(a_out.shape[1] // 128):
-        here = (lane // 32 + 4 * t) == h
-        pull = pull + jnp.where(here, shears[:, 128 * t : 128 * (t + 1)], 0.0)
-    pull = pull + pltpu.roll(pull, 64, 1)
-    pull = pull + pltpu.roll(pull, 32, 1)
+    shears_high, shears_low = split(shears)
+    pull = jnp.dot(
+        jnp.concatenate([shears_high, shears_low], axis=1), chosen, preferred_element_type=F32
+    )
     u_new = on_surface(free, surface_force(pull * weight))
     u, u_old = u_new, u
     put_rims(1, u.reshape(3 * nz, 8, 128))
@@ -606,7 +624,7 @@
             value = value + gram[c, d] * home_base[d]
         later.append(value)
     later = jnp.where(part < 8, later[0], jnp.where(part < 16, later[1], later[2]))
-    force = surface_force(later * weight)
+    force = surface_force(halves(later * weight))
 
     left_high, left_low = split(words)
     blank = [jnp.zeros((64, shears.shape[1]), F32)]
@@ -617,9 +635,9 @@
     moved = moved + jnp.dot(left_low, right_high, preferred_element_type=F32)
     moved = moved + jnp.dot(left_high, right_low, preferred_element_type=F32)
     moved_lane = iota(moved.shape, 1)
-    moved_row = iota(moved.shape, 0) // capacity * 32
+    moved_row = iota(moved.shape, 0) // capacity * 16
     moved = [
-        jnp.sum(jnp.where(moved_lane == moved_row + 8 * c, moved, 0.0), axis=1, keepdims=True)
+        jnp.sum(jnp.where(moved_lane == moved_row + 4 * c, moved, 0.0), axis=1, keepdims=True)
         for c in range(3)
     ]
     q_free = 2.0 * q - q_old + dt2 * (drive_of(moved) - stiff)
@@ -691,13 +709,14 @@
             pltpu.VMEM((2, pairs[0], 8, 128), F32),
             pltpu.VMEM((2, pairs[1], 8, 128), F32),
             pltpu.VMEM((STEPS, 2, 8, 128), F32),
-            pltpu.VMEM((STEPS, len(Y_DIRS), 2, 8, 128), F32),
-            pltpu.VMEM((capacity, a_width), F32),
-            pltpu.VMEM((owners, capacity, a_width), F32),
+            pltpu.VMEM((STEPS, 2, 8, 128), F32),
+            pltpu.VMEM((STEPS, 2, 8, 128), F32),
+            pltpu.VMEM((8, a_width), F32),
+            pltpu.VMEM((owners, 8, a_width), F32),
             pltpu.VMEM((owners, capacity, w_width), F32),
             pltpu.VMEM((owners, capacity, w_width), F32),
-            pltpu.VMEM((owners, capacity, 128), F32),
-            pltpu.VMEM((owners, capacity, 128), F32),
+            pltpu.VMEM((owners, 8, 128), F32),
+            pltpu.VMEM((owners, 8, 128), F32),
             pltpu.VMEM((kinds * freedoms, 2 * freedoms), BF16),
         ]
         + [pltpu.VMEM(operand.shape, operand.dtype) for operand in operands]

time: 14.7 us -> 14.2 us (0.966)
  the two profiles are of different devices: /device:TPU:3 before, /device:TPU:1 now
where the time goes in v2:
time: 14.2 us; the launch traced here: 14 us
  Pallas kernels  13.4 us (94%)
  between operations  0.64 us (5%)
    pallas_call x1, Pallas kernels, shards(): pl.pallas_call(functools.partial(kernel, rows, owners), out_shape=tuple((...  12.7 us
    pallas_call x1, Pallas kernels, shards(): pl.pallas_call(store, out_shape=results, in_specs=[vmem] * 4, out_specs=(...  0.71 us

profile of v2, /device:TPU:1, one launch (start us, length us, event | category | flops | bytes accessed | tf_op | source)
XLA Modules:
  0.0 14.0 jit_solution(1869732653045704260)
XLA Ops:
  0.6 12.7 %shard_map.147 = (f32[3,6,8,128]{3,2,1,0:T(8,128)S(1)}, f32[3,6,8,128]{3,2,1,0:T(8,128)S(1)}, f32[64,128]{1,0:T(8,128)S(1)}, f32[64,128]{1,0:T(8,128)S(1)}) custom-call(f32[3,6,8,128]{3,2,1,0:T(8,128)} %u_hbm.1, f32[3,6,8,128]{3,2,1,0:T(8,128)} %u_prev_hbm.1, f32[6,8,128]{2,1,0:T(8,128)} %lam_hbm.1, f32[6,8,128]{2,1,0:T(8,128)} %mu_hbm.1, ...), custom_call_target="tpu_custom_call" | custom-call | tf_op jit(solution)/shard_map/pallas_call | solution.py:701
  13.3 0.7 %shard_map.148 = (f32[3,6,8,128]{3,2,1,0:T(8,128)}, f32[3,6,8,128]{3,2,1,0:T(8,128)}, f32[64,128]{1,0:T(8,128)}, f32[64,128]{1,0:T(8,128)}) custom-call(f32[3,6,8,128]{3,2,1,0:T(8,128)S(1)} %get-tuple-element.8.refs_0_, f32[3,6,8,128]{3,2,1,0:T(8,128)S(1)} %get-tuple-element.9.refs_1_, f32[64,128]{1,0:T(8,128)S(1)} %get-tuple-element.10.refs_2_, ...), custom_call_target="tpu_custom_call" | custom-call | tf_op jit(solution)/shard_map/pallas_call | solution.py:737

commit v3 on v2

--- a/solution.py
+++ b/solution.py
@@ -156,33 +156,23 @@
     p_out,
     p_in,
     table,
-    u_ref,
-    u_prev_ref,
-    lam_ref,
-    mu_ref,
-    buoy_ref,
-    q_ref,
-    q_prev_ref,
+    frame_ref,
+    near_ref,
+    wide_ref,
+    far_ref,
     arch_ref,
-    stiff_ref,
-    couple_ref,
     counts_ref,
     cells_ref,
     loaded,
-    x_send,
-    x_recv,
-    y_send,
-    y_recv,
-    b_send,
-    b_recv,
+    sent,
+    arrived,
     entered,
 ):
     r, h = lax.axis_index("gx"), lax.axis_index("gy")
-    nz = lam_ref.shape[0]
-    slots = q_ref.shape[0]
+    nz = lam_hbm.shape[0]
+    slots, freedoms = q_hbm.shape
     capacity = slots // owners
-    kinds = stiff_ref.shape[0]
-    freedoms = q_ref.shape[1]
+    kinds = couple_hbm.shape[0] // 3
     dt2 = TIME_STEP * TIME_STEP
     xs, xr = (xs0, xs1), (xr0, xr1)
 
@@ -200,20 +190,20 @@
 
     loads = {}
 
-    def start_loads(pairs):
-        for source_ref, ref in pairs:
-            copy = pltpu.make_async_copy(source_ref, ref, loaded.at[len(loads)])
-            copy.start()
-            loads[id(ref)] = copy
-
-    start_loads(
-        (
-            (q_hbm, q_ref),
-            (couple_hbm, couple_ref),
-            (arch_hbm, arch_ref),
-            (u_hbm, u_ref),
-        )
-    )
+    def start_load(name, ref, parts):
+        sem = loaded.at[len(loads)]
+        start, places = 0, {}
+        for part, source_ref in parts:
+            size = source_ref.shape[0]
+            into = ref if len(parts) == 1 else ref.at[pl.ds(start, size)]
+            pltpu.make_async_copy(source_ref, into, sem).start()
+            places[part] = into
+            start += size
+        loads[name] = [pltpu.make_async_copy(ref, ref, sem)], places
+
+    start_load("frame", frame_ref, (("q", q_hbm), ("couple", couple_hbm)))
+    start_load("arch", arch_ref, (("arch", arch_hbm),))
+    start_load("near", near_ref, (("u", u_hbm), ("lam", lam_hbm), ("mu", mu_hbm)))
     peers = X_DIRS + tuple(d for d in Y_DIRS if d[0])
 
     barrier = pltpu.get_barrier_semaphore()
@@ -233,18 +223,10 @@
         def _(device=device):
             pl.semaphore_signal(barrier, inc=1, device_id=device, device_id_type=MESH)
 
-    start_loads(
-        (
-            (lam_hbm, lam_ref),
-            (mu_hbm, mu_ref),
-            (stiff_hbm, stiff_ref),
-            (q_prev_hbm, q_prev_ref),
-            (cells_hbm, cells_ref),
-            (counts_hbm, counts_ref),
-            (buoy_hbm, buoy_ref),
-            (u_prev_hbm, u_prev_ref),
-        )
-    )
+    start_load("cells", cells_ref, (("cells", cells_hbm),))
+    start_load("counts", counts_ref, (("counts", counts_hbm),))
+    start_load("far", far_ref, (("u_prev", u_prev_hbm), ("buoy", buoy_hbm)))
+    start_load("wide", wide_ref, (("stiff", stiff_hbm), ("q_prev", q_prev_hbm)))
 
     def half(ref, dx):
         return ref if dx == 0 else ref.at[pl.ds(RIM if dx > 0 else 0, RIM)]
@@ -271,16 +253,35 @@
                 ref = y_place(turn, direction)
                 ref[...] = jnp.zeros(ref.shape, F32)
 
-    def load(ref):
-        loads[id(ref)].wait()
-        return ref[...]
+    def load(part):
+        for copies, places in loads.values():
+            if part in places:
+                while copies:
+                    copies.pop().wait()
+                return places[part]
+
+    def wait_rows(sem, count):
+        rows_of = wide_ref.at[pl.ds(0, count)]
+        pltpu.make_async_copy(rows_of, rows_of, sem).wait()
+
+    def wait_rows_of_rims(sem, turns):
+        for nx in (1, 2):
+            for ny in (1, 2):
+                count = 0
+                for turn in turns:
+                    count += nx * xs[turn].shape[1] * 8 + ny * 8 + nx * ny * RIM
+                sides = [target(d)[0].astype(jnp.int32) for d in X_DIRS + ((0, 1), (0, -1))]
+
+                @pl.when((sides[0] + sides[1] == nx) & (sides[2] + sides[3] == ny))
+                def _(count=count):
+                    wait_rows(sem, count)
 
     def x_copy(turn, slot, device):
         return pltpu.make_async_remote_copy(
             src_ref=xs[turn].at[slot],
             dst_ref=xr[turn].at[slot],
-            send_sem=x_send.at[turn, slot],
-            recv_sem=x_recv.at[turn, slot],
+            send_sem=sent.at[0],
+            recv_sem=arrived.at[turn],
             device_id=device,
             device_id_type=MESH,
         )
@@ -289,8 +290,8 @@
         return pltpu.make_async_remote_copy(
             src_ref=half(ys.at[turn, 0 if Y_DIRS[slot][1] > 0 else 1], Y_DIRS[slot][0]),
             dst_ref=y_place(turn, Y_DIRS[slot]),
-            send_sem=y_send.at[turn, slot],
-            recv_sem=y_recv.at[turn, slot],
+            send_sem=sent.at[0],
+            recv_sem=arrived.at[turn],
             device_id=device,
             device_id_type=MESH,
         )
@@ -303,20 +304,8 @@
         return pltpu.make_async_remote_copy(
             src_ref=out if which == 0 else out.at[other],
             dst_ref=into.at[h],
-            send_sem=b_send.at[which, step],
-            recv_sem=b_recv.at[which, step],
-            device_id=(r, other),
-            device_id_type=MESH,
-        )
-
-    def b_arrival(which, step):
-        other = lax.rem(h + owners - step, owners)
-        out, into = messages[which]
-        return pltpu.make_async_remote_copy(
-            src_ref=out if which == 0 else out.at[other],
-            dst_ref=into.at[other],
-            send_sem=b_send.at[which, step],
-            recv_sem=b_recv.at[which, step],
+            send_sem=sent.at[1],
+            recv_sem=arrived.at[STEPS + which],
             device_id=(r, other),
             device_id_type=MESH,
         )
@@ -331,27 +320,14 @@
                     copy(turn, slot, device).start()
 
     def wait_rims(turn):
-        for copy, dirs in ((x_copy, X_DIRS), (y_copy, Y_DIRS)):
-            for slot, direction in enumerate(dirs):
-                there, device = source(direction)
-
-                @pl.when(there)
-                def _(copy=copy, slot=slot, device=device):
-                    copy(turn, slot, device).wait_recv()
+        wait_rows_of_rims(arrived.at[turn], (turn,))
 
     def wait_sends():
-        for turn in range(STEPS):
-            for copy, dirs in ((x_copy, X_DIRS), (y_copy, Y_DIRS)):
-                for slot, direction in enumerate(dirs):
-                    there, device = target(direction)
-
-                    @pl.when(there)
-                    def _(copy=copy, slot=slot, device=device, turn=turn):
-                        copy(turn, slot, device).wait_send()
-
-        for which in range(len(messages)):
-            for step in range(1, owners):
-                b_copy(which, step).wait_send()
+        wait_rows_of_rims(sent.at[0], range(STEPS))
+        size = 0
+        for out, into in messages:
+            size += into.shape[1] * into.shape[2] // 128
+        wait_rows(sent.at[1], (owners - 1) * size)
 
     def put_rims(turn, fields):
         to_next, to_before = pack_x(fields)
@@ -371,9 +347,10 @@
                 b_copy(which, owners - step).start()
 
     def take_buildings(which):
-        for step in range(1, owners):
-            b_arrival(which, step).wait_recv()
-        into = messages[which][1][...]
+        into = messages[which][1]
+        others = into.at[pl.ds(0, owners - 1)]
+        pltpu.make_async_copy(others, others, arrived.at[STEPS + which]).wait()
+        into = into[...]
         if into.shape[1] < capacity:
             into = jnp.concatenate([into, pltpu.roll(into, into.shape[2] // 2, 2)], axis=1)
         return into.reshape(slots, into.shape[2])
@@ -383,9 +360,9 @@
     slot_row = iota((slots, 1), 0)
     square = (slots, slots)
 
-    couple = load(couple_ref)
+    couple = load("couple")[...].reshape(3, kinds, freedoms)
     arch = jnp.sum(
-        jnp.where(iota(square, 0) == iota(square, 1), load(arch_ref).astype(F32), 0.0),
+        jnp.where(iota(square, 0) == iota(square, 1), load("arch")[...].astype(F32), 0.0),
         axis=1,
         keepdims=True,
     )
@@ -400,7 +377,7 @@
     def couple_sum(c, state):
         return jnp.sum(coupling[c] * state, axis=1, keepdims=True)
 
-    q = load(q_ref)
+    q = load("q")[...]
     shear = [couple_sum(c, q) for c in range(3)]
     word = lane & 15
     shear = jnp.where(word < 4, shear[0], jnp.where(word < 8, shear[1], shear[2]))
@@ -416,8 +393,8 @@
         a_out[:, 128 * t : 128 * (t + 1)] = tile
     a_in[h] = a_out[...]
 
-    u = load(u_ref)
-    lam, mu = load(lam_ref) * (1.0 / 144.0), load(mu_ref) * (1.0 / 144.0)
+    u = load("u")[...].reshape(3, nz, 8, 128)
+    lam, mu = load("lam")[...] * (1.0 / 144.0), load("mu")[...] * (1.0 / 144.0)
     put_rims(0, jnp.concatenate([u.reshape(3 * nz, 8, 128), lam, mu], axis=0))
     pl.semaphore_wait(barrier, arrivals)
     for step in range(1, owners - 1):
@@ -426,7 +403,7 @@
         @pl.when(h + step >= owners)
         def _(step=step, other=other):
             pl.semaphore_signal(
-                entered.at[owners - step], inc=1, device_id=(r, other), device_id_type=MESH
+                entered.at[owners - step - 2], inc=1, device_id=(r, other), device_id_type=MESH
             )
 
     for step in range(1, owners):
@@ -437,7 +414,7 @@
 
     send_rims(0)
 
-    cells = load(cells_ref)[0].astype(F32)
+    cells = load("cells")[0].astype(F32)
     wide = (slots, slots * FOOTPRINT_CELLS)
     own = (iota(wide, 1) // FOOTPRINT_CELLS) == iota(wide, 0)
     corner_cell = jnp.min(jnp.where(own, cells, 1e9), axis=1, keepdims=True)
@@ -447,8 +424,7 @@
     in_y = ((along_y == 0.0) | (along_y == 1.0)).astype(F32)
     window_y = in_y.astype(BF16)
     along_x = (lane & 7).astype(F32) - corner_x
-    loads[id(counts_ref)].wait()
-    row_counts = counts_ref[0, pl.ds(h, 1), :].astype(F32)
+    row_counts = load("counts")[0, pl.ds(h, 1), :].astype(F32)
     pairs = (slots, owners)
     live_count = jnp.sum(
         jnp.where(iota(pairs, 0) // capacity == iota(pairs, 1), row_counts, 0.0),
@@ -510,7 +486,7 @@
     base = surface_motion(u)
     home_base = [group_sum(c, base) for c in range(3)]
 
-    gain = load(buoy_ref) * dt2
+    gain = load("buoy")[...] * dt2
     overlap_left, overlap_right = [], []
     for x in range(8):
         there = live & ((corner_x == float(x)) | (corner_x == float(x - 1)))
@@ -528,10 +504,10 @@
     overlap = lax.dot_general(left_high, right, nt, preferred_element_type=F32)
     overlap = overlap + lax.dot_general(left_low, right, nt, preferred_element_type=F32)
 
-    stiff_high, stiff_low = split(load(stiff_ref).reshape(kinds * freedoms, freedoms))
+    stiff_high, stiff_low = split(load("stiff")[...])
     table[:, :freedoms] = stiff_high
     table[:, freedoms:] = stiff_low
-    coasting = 2.0 * q - load(q_prev_ref) - dt2 * stiff_term(q)
+    coasting = 2.0 * q - load("q_prev")[...] - dt2 * stiff_term(q)
     fields = base
     columns = [couple_sum(c, coasting) for c in range(3)]
     pairs_of = ((0, 0), (0, 1), (0, 2), (1, 1), (1, 2), (2, 2))
@@ -548,12 +524,12 @@
 
         @pl.when(h + step < owners)
         def _(step=step):
-            pl.semaphore_wait(entered.at[step], 1)
+            pl.semaphore_wait(entered.at[step - 2], 1)
             b_copy(0, step).start()
 
     send_buildings(1)
 
-    u_old = load(u_prev_ref)
+    u_old = load("u_prev")[...].reshape(3, nz, 8, 128)
 
     shape = (3, nz, 8, 128)
 
@@ -678,17 +654,18 @@
     vmem = pl.BlockSpec(memory_space=pltpu.VMEM)
     hbm = pl.BlockSpec(memory_space=pltpu.HBM)
     dma = pltpu.SemaphoreType.DMA
+    tiles = (3 * nz, 8, 128)
     operands = (
-        u_now,
-        u_prev,
+        u_now.reshape(tiles),
+        u_prev.reshape(tiles),
         lame_lambda,
         lame_mu,
         buoyancy,
         q_now,
         q_prev,
         archetype.reshape(1, slots),
-        stiffness,
-        couple.transpose(1, 0, 2),
+        stiffness.reshape(kinds * freedoms, freedoms),
+        couple.transpose(1, 0, 2).reshape(3 * kinds, freedoms),
         counts,
         footprint,
     )
@@ -719,16 +696,18 @@
             pltpu.VMEM((owners, 8, 128), F32),
             pltpu.VMEM((kinds * freedoms, 2 * freedoms), BF16),
         ]
-        + [pltpu.VMEM(operand.shape, operand.dtype) for operand in operands]
         + [
-            dma((len(operands),)),
-            dma((STEPS, 2)),
-            dma((STEPS, 2)),
-            dma((STEPS, len(Y_DIRS))),
-            dma((STEPS, len(Y_DIRS))),
-            dma((3, owners)),
-            dma((3, owners)),
-            pltpu.SemaphoreType.REGULAR((owners,)),
+            pltpu.VMEM((slots + 3 * kinds, freedoms), F32),
+            pltpu.VMEM((5 * nz, 8, 128), F32),
+            pltpu.VMEM((kinds * freedoms + slots, freedoms), F32),
+            pltpu.VMEM((4 * nz, 8, 128), F32),
+            pltpu.VMEM((1, slots), jnp.int32),
+            pltpu.VMEM(counts.shape, jnp.int32),
+            pltpu.VMEM(footprint.shape, jnp.int32),
+            dma((7,)),
+            dma((2,)),
+            dma((STEPS + 3,)),
+            pltpu.SemaphoreType.REGULAR((owners - 2,)),
         ],
         compiler_params=pltpu.CompilerParams(
             collective_id=0, has_side_effects=True, vmem_limit_bytes=60 * 1024 * 1024

time: 14.2 us -> 13.7 us (0.965)
  Pallas kernels: 13.4 us -> 12.9 us
    pallas_call x1, Pallas kernels: 12.7 us -> 12.2 us  [shards(): pl.pallas_call(functools.partial(kernel, rows, owners), out_shape=tuple((...]
where the time goes in v3:
time: 13.7 us; the launch traced here: 13.5 us
  Pallas kernels  12.9 us (94%)
  between operations  0.64 us (5%)
    pallas_call x1, Pallas kernels, shards(): pl.pallas_call(functools.partial(kernel, rows, owners), out_shape=tuple((...  12.2 us
    pallas_call x1, Pallas kernels, shards(): pl.pallas_call(store, out_shape=results, in_specs=[vmem] * 4, out_specs=(...  0.71 us

profile of v3, /device:TPU:1, one launch (start us, length us, event | category | flops | bytes accessed | tf_op | source)
XLA Modules:
  0.0 13.5 jit_solution(7535226932115273954)
XLA Ops:
  0.6 12.2 %shard_map.147 = (f32[3,6,8,128]{3,2,1,0:T(8,128)S(1)}, f32[3,6,8,128]{3,2,1,0:T(8,128)S(1)}, f32[64,128]{1,0:T(8,128)S(1)}, f32[64,128]{1,0:T(8,128)S(1)}) custom-call(f32[18,8,128]{2,1,0:T(8,128)} %bitcast.8, f32[18,8,128]{2,1,0:T(8,128)} %bitcast.9, f32[6,8,128]{2,1,0:T(8,128)} %lam_hbm.1, f32[6,8,128]{2,1,0:T(8,128)} %mu_hbm.1, f32[6,8,128]{2,1,0:T(8,128)} %buoy_hbm.1, ...), custom_call_target="tpu_custom_call" | custom-call | tf_op jit(solution)/shard_map/pallas_call | solution.py:678
  12.8 0.7 %shard_map.148 = (f32[3,6,8,128]{3,2,1,0:T(8,128)}, f32[3,6,8,128]{3,2,1,0:T(8,128)}, f32[64,128]{1,0:T(8,128)}, f32[64,128]{1,0:T(8,128)}) custom-call(f32[3,6,8,128]{3,2,1,0:T(8,128)S(1)} %get-tuple-element.8.refs_0_, f32[3,6,8,128]{3,2,1,0:T(8,128)S(1)} %get-tuple-element.9.refs_1_, f32[64,128]{1,0:T(8,128)S(1)} %get-tuple-element.10.refs_2_, ...), custom_call_target="tpu_custom_call" | custom-call | tf_op jit(solution)/shard_map/pallas_call | solution.py:716

commit v4 on v3

--- a/solution.py
+++ b/solution.py
@@ -17,6 +17,8 @@
 
 X_DIRS = ((1, 0), (-1, 0))
 Y_DIRS = ((-1, 1), (-1, -1), (0, 1), (0, -1), (1, 1), (1, -1))
+DIRS = X_DIRS + Y_DIRS
+HEARD = tuple(d for d in DIRS if d[1] > 0 or d in X_DIRS)
 
 
 def iota(shape, dim):
@@ -204,24 +206,41 @@
     start_load("frame", frame_ref, (("q", q_hbm), ("couple", couple_hbm)))
     start_load("arch", arch_ref, (("arch", arch_hbm),))
     start_load("near", near_ref, (("u", u_hbm), ("lam", lam_hbm), ("mu", mu_hbm)))
-    peers = X_DIRS + tuple(d for d in Y_DIRS if d[0])
+    odd = lax.rem(r, 2) == 1
+    even = jnp.logical_not(odd)
+
+    def later(direction):
+        dx, dy = direction
+        there = target(direction)[0]
+        if dy == 0 or direction == (-1, 1):
+            return there & odd
+        return there if dy > 0 else None
+
+    def earlier(direction):
+        dx, dy = direction
+        there = target(direction)[0]
+        if dy == 0 or direction == (1, -1):
+            return there & even
+        return there if dy < 0 else None
 
     barrier = pltpu.get_barrier_semaphore()
-    arrivals = h + (h + 1 < owners).astype(jnp.int32)
-    for step in range(1, owners):
-        other = lax.rem(h + step, owners)
-
-        @pl.when((h + step < owners) | (step == owners - 1))
-        def _(other=other):
-            pl.semaphore_signal(barrier, inc=1, device_id=(r, other), device_id_type=MESH)
-
-    for direction in peers:
-        there, device = target(direction)
-        arrivals = arrivals + there.astype(jnp.int32)
-
-        @pl.when(there)
-        def _(device=device):
+    for direction in DIRS:
+        if later(direction) is not None:
+
+            @pl.when(later(direction))
+            def _(device=target(direction)[1]):
+                pl.semaphore_signal(barrier, inc=1, device_id=device, device_id_type=MESH)
+
+    for step in range(2, owners):
+
+        @pl.when(h + step < owners)
+        def _(device=(r, h + step)):
             pl.semaphore_signal(barrier, inc=1, device_id=device, device_id_type=MESH)
+
+    arrivals = jnp.maximum(h - 1, 0)
+    for direction in DIRS:
+        if earlier(direction) is not None:
+            arrivals = arrivals + earlier(direction).astype(jnp.int32)
 
     start_load("cells", cells_ref, (("cells", cells_hbm),))
     start_load("counts", counts_ref, (("counts", counts_hbm),))
@@ -252,6 +271,36 @@
             for turn in range(STEPS):
                 ref = y_place(turn, direction)
                 ref[...] = jnp.zeros(ref.shape, F32)
+
+    @pl.when(arrivals > 0)
+    def _():
+        pl.semaphore_wait(barrier, arrivals)
+
+    def tell(direction, about):
+        pl.semaphore_signal(
+            entered.at[HEARD.index(about)],
+            inc=1,
+            device_id=target(direction)[1],
+            device_id_type=MESH,
+        )
+
+    for direction in DIRS:
+        if earlier(direction) is not None:
+
+            @pl.when(earlier(direction))
+            def _(direction=direction):
+                tell(direction, (-direction[0], -direction[1]))
+
+    for step in range(2, owners):
+
+        @pl.when(h >= step)
+        def _(step=step):
+            pl.semaphore_signal(
+                entered.at[len(HEARD) + step - 2],
+                inc=1,
+                device_id=(r, h - step),
+                device_id_type=MESH,
+            )
 
     def load(part):
         for copies, places in loads.values():
@@ -310,14 +359,22 @@
             device_id_type=MESH,
         )
 
+    def rim_copy(turn, direction):
+        _, device = target(direction)
+        if direction in X_DIRS:
+            return x_copy(turn, X_DIRS.index(direction), device)
+        return y_copy(turn, Y_DIRS.index(direction), device)
+
+    def send_rim(turn, direction):
+        there, _ = target(direction)
+
+        @pl.when(there)
+        def _():
+            rim_copy(turn, direction).start()
+
     def send_rims(turn):
-        for copy, dirs in ((x_copy, X_DIRS), (y_copy, Y_DIRS)):
-            for slot, direction in enumerate(dirs):
-                there, device = target(direction)
-
-                @pl.when(there)
-                def _(copy=copy, slot=slot, device=device):
-                    copy(turn, slot, device).start()
+        for direction in X_DIRS + Y_DIRS:
+            send_rim(turn, direction)
 
     def wait_rims(turn):
         wait_rows_of_rims(arrived.at[turn], (turn,))
@@ -396,23 +453,28 @@
     u = load("u")[...].reshape(3, nz, 8, 128)
     lam, mu = load("lam")[...] * (1.0 / 144.0), load("mu")[...] * (1.0 / 144.0)
     put_rims(0, jnp.concatenate([u.reshape(3 * nz, 8, 128), lam, mu], axis=0))
-    pl.semaphore_wait(barrier, arrivals)
-    for step in range(1, owners - 1):
-        other = lax.rem(h + step, owners)
+    for step in range(1, owners):
 
         @pl.when(h + step >= owners)
-        def _(step=step, other=other):
-            pl.semaphore_signal(
-                entered.at[owners - step - 2], inc=1, device_id=(r, other), device_id_type=MESH
-            )
-
-    for step in range(1, owners):
-
-        @pl.when((h + step >= owners) | (step == 1))
         def _(step=step):
             b_copy(0, step).start()
 
-    send_rims(0)
+    for direction in DIRS:
+        if earlier(direction) is not None:
+
+            @pl.when(earlier(direction))
+            def _(direction=direction):
+                rim_copy(0, direction).start()
+
+    def send_later(direction, when):
+        @pl.when(when)
+        def _():
+            pl.semaphore_wait(entered.at[HEARD.index(direction)], 1)
+            if direction == (0, 1):
+                b_copy(0, 1).start()
+            rim_copy(0, direction).start()
+
+    send_later((-1, 0), later((-1, 0)))
 
     cells = load("cells")[0].astype(F32)
     wide = (slots, slots * FOOTPRINT_CELLS)
@@ -504,6 +566,15 @@
     overlap = lax.dot_general(left_high, right, nt, preferred_element_type=F32)
     overlap = overlap + lax.dot_general(left_low, right, nt, preferred_element_type=F32)
 
+    send_later((1, 0), later((1, 0)))
+    send_later((0, 1), later((0, 1)))
+
+    for direction, side in (((1, -1), odd), ((-1, 1), even)):
+
+        @pl.when(target(direction)[0] & side)
+        def _(direction=direction):
+            rim_copy(0, direction).start()
+
     stiff_high, stiff_low = split(load("stiff")[...])
     table[:, :freedoms] = stiff_high
     table[:, freedoms:] = stiff_low
@@ -520,11 +591,13 @@
         first = jnp.concatenate([first, overlap[:, 128:]], axis=1)
     w_out[...] = first.reshape(owners, capacity, width)
     w_in[h] = w_out[h]
+    send_later((-1, 1), later((-1, 1)))
+    send_later((1, 1), later((1, 1)))
     for step in range(2, owners):
 
         @pl.when(h + step < owners)
         def _(step=step):
-            pl.semaphore_wait(entered.at[step - 2], 1)
+            pl.semaphore_wait(entered.at[len(HEARD) + step - 2], 1)
             b_copy(0, step).start()
 
     send_buildings(1)
@@ -533,25 +606,9 @@
 
     shape = (3, nz, 8, 128)
 
-    def push(turn, field, lam_mu):
-        count = (5 if turn == 0 else 3) * nz
-        rim_x, rim_y, corner = take_rims(turn, count)
-        if turn == 0:
-            lam_mu = rim_x[3 * nz :], rim_y[3 * nz :]
-        lam_mu_x, lam_mu_y = lam_mu
-        total = divergence(
-            field,
-            rim_x[: 3 * nz].reshape(shape),
-            rim_y[: 3 * nz].reshape(shape),
-            corner.reshape(shape),
-            lam,
-            mu,
-            lam_mu_x[:nz],
-            lam_mu_x[nz:],
-            lam_mu_y[:nz],
-            lam_mu_y[nz:],
-        )
-        return total, lam_mu
+    def push(field, rims, lam_mu, levels):
+        fields = [part.reshape(shape)[:, :levels] for part in (field,) + rims]
+        return divergence(*fields, *[part[:levels] for part in (lam, mu) + lam_mu])
 
     def on_surface(field, force):
         return jnp.concatenate([field[:, :1] + (gain[0] * force)[:, None], field[:, 1:]], axis=1)
@@ -563,14 +620,22 @@
     chosen = ((place == word) & (column < 64) & ((column & 31) < 24)).astype(F32).astype(BF16)
 
     wait_rims(0)
-    total, lam_mu = push(0, u, None)
-    free = 2.0 * u - u_old + gain * total
-    motion = surface_motion(free).reshape(owners, 2, 8, 128)
+    rim_x, rim_y, corner = take_rims(0, 5 * nz)
+    lam_mu = rim_x[3 * nz : 4 * nz], rim_x[4 * nz :], rim_y[3 * nz : 4 * nz], rim_y[4 * nz :]
+    rims = rim_x[: 3 * nz], rim_y[: 3 * nz], corner
+    coast = 2.0 * u - u_old
+    top = push(u, rims, lam_mu, min(nz, 5))[:, :1]
+    motion = surface_motion(coast[:, :1] + gain[:1] * top).reshape(owners, 2, 8, 128)
     p_out[...] = jnp.where(
         iota((owners, 8, 128), 2) < 64, motion[:, 0], pltpu.roll(motion[:, 1], 64, 2)
     )
     p_in[h] = p_out[h]
-    send_buildings(2)
+
+    @pl.when(h >= 0)
+    def _():
+        send_buildings(2)
+
+    free = coast + gain * push(u, rims, lam_mu, nz)
 
     shears = take_buildings(0)
     shears_high, shears_low = split(shears)
@@ -620,7 +685,7 @@
     u_free = on_surface(2.0 * u - u_old, force)
 
     wait_rims(1)
-    total, _ = push(1, u, lam_mu)
+    total = push(u, take_rims(1, 3 * nz), lam_mu, nz)
     u_last_ref[...] = u_free + gain * total
 
     motion = take_buildings(2)
@@ -707,7 +772,7 @@
             dma((7,)),
             dma((2,)),
             dma((STEPS + 3,)),
-            pltpu.SemaphoreType.REGULAR((owners - 2,)),
+            pltpu.SemaphoreType.REGULAR((len(HEARD) + owners - 2,)),
         ],
         compiler_params=pltpu.CompilerParams(
             collective_id=0, has_side_effects=True, vmem_limit_bytes=60 * 1024 * 1024

time: 13.7 us -> 13.3 us (0.971)
  Pallas kernels: 12.9 us -> 12.6 us
    pallas_call x1, Pallas kernels: 12.2 us -> 11.8 us  [shards(): pl.pallas_call(functools.partial(kernel, rows, owners), out_shape=tuple((...]
where the time goes in v4:
time: 13.3 us; the launch traced here: 13.2 us
  Pallas kernels  12.6 us (95%)
  between operations  0.64 us (5%)
    pallas_call x1, Pallas kernels, shards(): pl.pallas_call(functools.partial(kernel, rows, owners), out_shape=tuple((...  11.8 us
    pallas_call x1, Pallas kernels, shards(): pl.pallas_call(store, out_shape=results, in_specs=[vmem] * 4, out_specs=(...  0.71 us

profile of v4, /device:TPU:1, one launch (start us, length us, event | category | flops | bytes accessed | tf_op | source)
XLA Modules:
  0.0 13.2 jit_solution(13425187685413031984)
XLA Ops:
  0.6 11.8 %shard_map.147 = (f32[3,6,8,128]{3,2,1,0:T(8,128)S(1)}, f32[3,6,8,128]{3,2,1,0:T(8,128)S(1)}, f32[64,128]{1,0:T(8,128)S(1)}, f32[64,128]{1,0:T(8,128)S(1)}) custom-call(f32[18,8,128]{2,1,0:T(8,128)} %bitcast.8, f32[18,8,128]{2,1,0:T(8,128)} %bitcast.9, f32[6,8,128]{2,1,0:T(8,128)} %lam_hbm.1, f32[6,8,128]{2,1,0:T(8,128)} %mu_hbm.1, f32[6,8,128]{2,1,0:T(8,128)} %buoy_hbm.1, ...), custom_call_target="tpu_custom_call" | custom-call | tf_op jit(solution)/shard_map/pallas_call | solution.py:743
  12.5 0.7 %shard_map.148 = (f32[3,6,8,128]{3,2,1,0:T(8,128)}, f32[3,6,8,128]{3,2,1,0:T(8,128)}, f32[64,128]{1,0:T(8,128)}, f32[64,128]{1,0:T(8,128)}) custom-call(f32[3,6,8,128]{3,2,1,0:T(8,128)S(1)} %get-tuple-element.8.refs_0_, f32[3,6,8,128]{3,2,1,0:T(8,128)S(1)} %get-tuple-element.9.refs_1_, f32[64,128]{1,0:T(8,128)S(1)} %get-tuple-element.10.refs_2_, ...), custom_call_target="tpu_custom_call" | custom-call | tf_op jit(solution)/shard_map/pallas_call | solution.py:781

commit v5 on v4

--- a/solution.py
+++ b/solution.py
@@ -255,23 +255,6 @@
         k = 0 if dy > 0 else 1
         return half((cr if dx else yr).at[turn, k], dx)
 
-    for slot, direction in enumerate(X_DIRS):
-        there, _ = source(direction)
-
-        @pl.when(jnp.logical_not(there))
-        def _(slot=slot):
-            for buffer in xr:
-                buffer[slot] = jnp.zeros(buffer.shape[1:], F32)
-
-    for slot, direction in enumerate(Y_DIRS):
-        there, _ = source(direction)
-
-        @pl.when(jnp.logical_not(there))
-        def _(direction=direction):
-            for turn in range(STEPS):
-                ref = y_place(turn, direction)
-                ref[...] = jnp.zeros(ref.shape, F32)
-
     @pl.when(arrivals > 0)
     def _():
         pl.semaphore_wait(barrier, arrivals)
@@ -301,6 +284,23 @@
                 device_id=(r, h - step),
                 device_id_type=MESH,
             )
+
+    for slot, direction in enumerate(X_DIRS):
+        there, _ = source(direction)
+
+        @pl.when(jnp.logical_not(there))
+        def _(slot=slot):
+            for buffer in xr:
+                buffer[slot] = jnp.zeros(buffer.shape[1:], F32)
+
+    for slot, direction in enumerate(Y_DIRS):
+        there, _ = source(direction)
+
+        @pl.when(jnp.logical_not(there))
+        def _(direction=direction):
+            for turn in range(STEPS):
+                ref = y_place(turn, direction)
+                ref[...] = jnp.zeros(ref.shape, F32)
 
     def load(part):
         for copies, places in loads.values():
@@ -449,16 +449,15 @@
                 tile = jnp.where(group == k, shear[home, which], tile)
         a_out[:, 128 * t : 128 * (t + 1)] = tile
     a_in[h] = a_out[...]
+    for step in range(1, owners):
+
+        @pl.when(h + step >= owners)
+        def _(step=step):
+            b_copy(0, step).start()
 
     u = load("u")[...].reshape(3, nz, 8, 128)
     lam, mu = load("lam")[...] * (1.0 / 144.0), load("mu")[...] * (1.0 / 144.0)
     put_rims(0, jnp.concatenate([u.reshape(3 * nz, 8, 128), lam, mu], axis=0))
-    for step in range(1, owners):
-
-        @pl.when(h + step >= owners)
-        def _(step=step):
-            b_copy(0, step).start()
-
     for direction in DIRS:
         if earlier(direction) is not None:
 
@@ -566,14 +565,16 @@
     overlap = lax.dot_general(left_high, right, nt, preferred_element_type=F32)
     overlap = overlap + lax.dot_general(left_low, right, nt, preferred_element_type=F32)
 
+    def send_corner(direction, side):
+        @pl.when(target(direction)[0] & side)
+        def _():
+            rim_copy(0, direction).start()
+
+    send_later((0, 1), later((0, 1)))
+    send_corner((-1, 1), even)
+    send_later((-1, 1), later((-1, 1)))
     send_later((1, 0), later((1, 0)))
-    send_later((0, 1), later((0, 1)))
-
-    for direction, side in (((1, -1), odd), ((-1, 1), even)):
-
-        @pl.when(target(direction)[0] & side)
-        def _(direction=direction):
-            rim_copy(0, direction).start()
+    send_corner((1, -1), odd)
 
     stiff_high, stiff_low = split(load("stiff")[...])
     table[:, :freedoms] = stiff_high
@@ -591,7 +592,6 @@
         first = jnp.concatenate([first, overlap[:, 128:]], axis=1)
     w_out[...] = first.reshape(owners, capacity, width)
     w_in[h] = w_out[h]
-    send_later((-1, 1), later((-1, 1)))
     send_later((1, 1), later((1, 1)))
     for step in range(2, owners):
 
@@ -612,12 +612,6 @@
 
     def on_surface(field, force):
         return jnp.concatenate([field[:, :1] + (gain[0] * force)[:, None], field[:, 1:]], axis=1)
-
-    picked = (2 * a_width, 128)
-    place, column = iota(picked, 0), iota(picked, 1)
-    word = 16 * h + 4 * ((column & 31) // 8)
-    word = jnp.where(column < 32, word, word + a_width)
-    chosen = ((place == word) & (column < 64) & ((column & 31) < 24)).astype(F32).astype(BF16)
 
     wait_rims(0)
     rim_x, rim_y, corner = take_rims(0, 5 * nz)
@@ -638,11 +632,12 @@
     free = coast + gain * push(u, rims, lam_mu, nz)
 
     shears = take_buildings(0)
-    shears_high, shears_low = split(shears)
-    pull = jnp.dot(
-        jnp.concatenate([shears_high, shears_low], axis=1), chosen, preferred_element_type=F32
-    )
-    u_new = on_surface(free, surface_force(pull * weight))
+    place = iota(shears.shape, 1) - 16 * h
+    first = [
+        jnp.sum(jnp.where(place == 4 * c, shears, 0.0), axis=1, keepdims=True) for c in range(3)
+    ]
+    pull = jnp.where(part < 8, first[0], jnp.where(part < 16, first[1], first[2]))
+    u_new = on_surface(free, surface_force(halves(pull * weight)))
     u, u_old = u_new, u
     put_rims(1, u.reshape(3 * nz, 8, 128))
     send_rims(1)

time: 13.3 us -> 13.3 us (level)
  no operation moved by 1% of the time
where the time goes in v5:
time: 13.3 us; the launch traced here: 13.1 us
  Pallas kernels  12.5 us (94%)
  between operations  0.64 us (5%)
    pallas_call x1, Pallas kernels, shards(): pl.pallas_call(functools.partial(kernel, rows, owners), out_shape=tuple((...  11.8 us
    pallas_call x1, Pallas kernels, shards(): pl.pallas_call(store, out_shape=results, in_specs=[vmem] * 4, out_specs=(...  0.71 us

profile of v5, /device:TPU:1, one launch (start us, length us, event | category | flops | bytes accessed | tf_op | source)
XLA Modules:
  0.0 13.1 jit_solution(15876019534346889844)
XLA Ops:
  0.6 11.8 %shard_map.147 = (f32[3,6,8,128]{3,2,1,0:T(8,128)S(1)}, f32[3,6,8,128]{3,2,1,0:T(8,128)S(1)}, f32[64,128]{1,0:T(8,128)S(1)}, f32[64,128]{1,0:T(8,128)S(1)}) custom-call(f32[18,8,128]{2,1,0:T(8,128)} %bitcast.8, f32[18,8,128]{2,1,0:T(8,128)} %bitcast.9, f32[6,8,128]{2,1,0:T(8,128)} %lam_hbm.1, f32[6,8,128]{2,1,0:T(8,128)} %mu_hbm.1, f32[6,8,128]{2,1,0:T(8,128)} %buoy_hbm.1, ...), custom_call_target="tpu_custom_call" | custom-call | tf_op jit(solution)/shard_map/pallas_call | solution.py:738
  12.4 0.7 %shard_map.148 = (f32[3,6,8,128]{3,2,1,0:T(8,128)}, f32[3,6,8,128]{3,2,1,0:T(8,128)}, f32[64,128]{1,0:T(8,128)}, f32[64,128]{1,0:T(8,128)}) custom-call(f32[3,6,8,128]{3,2,1,0:T(8,128)S(1)} %get-tuple-element.8.refs_0_, f32[3,6,8,128]{3,2,1,0:T(8,128)S(1)} %get-tuple-element.9.refs_1_, f32[64,128]{1,0:T(8,128)S(1)} %get-tuple-element.10.refs_2_, ...), custom_call_target="tpu_custom_call" | custom-call | tf_op jit(solution)/shard_map/pallas_call | solution.py:776

commit v6 on v5

--- a/solution.py
+++ b/solution.py
@@ -161,7 +161,6 @@
     frame_ref,
     near_ref,
     wide_ref,
-    far_ref,
     arch_ref,
     counts_ref,
     cells_ref,
@@ -244,8 +243,16 @@
 
     start_load("cells", cells_ref, (("cells", cells_hbm),))
     start_load("counts", counts_ref, (("counts", counts_hbm),))
-    start_load("far", far_ref, (("u_prev", u_prev_hbm), ("buoy", buoy_hbm)))
-    start_load("wide", wide_ref, (("stiff", stiff_hbm), ("q_prev", q_prev_hbm)))
+    start_load(
+        "wide",
+        wide_ref,
+        (
+            ("buoy", buoy_hbm),
+            ("stiff", stiff_hbm),
+            ("q_prev", q_prev_hbm),
+            ("u_prev", u_prev_hbm),
+        ),
+    )
 
     def half(ref, dx):
         return ref if dx == 0 else ref.at[pl.ds(RIM if dx > 0 else 0, RIM)]
@@ -313,10 +320,10 @@
         rows_of = wide_ref.at[pl.ds(0, count)]
         pltpu.make_async_copy(rows_of, rows_of, sem).wait()
 
-    def wait_rows_of_rims(sem, turns):
+    def wait_rows_of_rims(sem, turns, others=0):
         for nx in (1, 2):
             for ny in (1, 2):
-                count = 0
+                count = others
                 for turn in turns:
                     count += nx * xs[turn].shape[1] * 8 + ny * 8 + nx * ny * RIM
                 sides = [target(d)[0].astype(jnp.int32) for d in X_DIRS + ((0, 1), (0, -1))]
@@ -353,7 +360,7 @@
         return pltpu.make_async_remote_copy(
             src_ref=out if which == 0 else out.at[other],
             dst_ref=into.at[h],
-            send_sem=sent.at[1],
+            send_sem=sent.at[0],
             recv_sem=arrived.at[STEPS + which],
             device_id=(r, other),
             device_id_type=MESH,
@@ -380,11 +387,10 @@
         wait_rows_of_rims(arrived.at[turn], (turn,))
 
     def wait_sends():
-        wait_rows_of_rims(sent.at[0], range(STEPS))
         size = 0
         for out, into in messages:
             size += into.shape[1] * into.shape[2] // 128
-        wait_rows(sent.at[1], (owners - 1) * size)
+        wait_rows_of_rims(sent.at[0], range(STEPS), (owners - 1) * size)
 
     def put_rims(turn, fields):
         to_next, to_before = pack_x(fields)
@@ -547,7 +553,7 @@
     base = surface_motion(u)
     home_base = [group_sum(c, base) for c in range(3)]
 
-    gain = load("buoy")[...] * dt2
+    gain = load("buoy")[...].reshape(nz, 8, 128) * dt2
     overlap_left, overlap_right = [], []
     for x in range(8):
         there = live & ((corner_x == float(x)) | (corner_x == float(x - 1)))
@@ -679,12 +685,17 @@
     q_free = 2.0 * q - q_old + dt2 * (drive_of(moved) - stiff)
     u_free = on_surface(2.0 * u - u_old, force)
 
+    def finish_frames():
+        motion = take_buildings(2)
+        q_last_ref[...] = q_free + dt2 * drive_of([group_sum(c, motion) for c in range(3)])
+
+    rims_last = odd & (r + h > 1)
+    pl.when(rims_last)(finish_frames)
     wait_rims(1)
     total = push(u, take_rims(1, 3 * nz), lam_mu, nz)
     u_last_ref[...] = u_free + gain * total
 
-    motion = take_buildings(2)
-    q_last_ref[...] = q_free + dt2 * drive_of([group_sum(c, motion) for c in range(3)])
+    pl.when(jnp.logical_not(rims_last))(finish_frames)
     wait_sends()
 
 
@@ -717,10 +728,10 @@
     tiles = (3 * nz, 8, 128)
     operands = (
         u_now.reshape(tiles),
-        u_prev.reshape(tiles),
+        u_prev.reshape(3 * nz * 8, 128),
         lame_lambda,
         lame_mu,
-        buoyancy,
+        buoyancy.reshape(nz * 8, 128),
         q_now,
         q_prev,
         archetype.reshape(1, slots),
@@ -759,13 +770,12 @@
         + [
             pltpu.VMEM((slots + 3 * kinds, freedoms), F32),
             pltpu.VMEM((5 * nz, 8, 128), F32),
-            pltpu.VMEM((kinds * freedoms + slots, freedoms), F32),
-            pltpu.VMEM((4 * nz, 8, 128), F32),
+            pltpu.VMEM((kinds * freedoms + slots + 4 * nz * 8, freedoms), F32),
             pltpu.VMEM((1, slots), jnp.int32),
             pltpu.VMEM(counts.shape, jnp.int32),
             pltpu.VMEM(footprint.shape, jnp.int32),
-            dma((7,)),
-            dma((2,)),
+            dma((6,)),
+            dma((1,)),
             dma((STEPS + 3,)),
             pltpu.SemaphoreType.REGULAR((len(HEARD) + owners - 2,)),
         ],
@@ -778,19 +788,16 @@
         out_shape=results,
         in_specs=[vmem] * 4,
         out_specs=(hbm,) * 4,
-        scratch_shapes=[dma((4,))],
-        compiler_params=pltpu.CompilerParams(vmem_limit_bytes=1024 * 1024),
+        scratch_shapes=[pltpu.VMEM((2 * (3 * nz * 8 + slots), 128), F32), dma((1,))],
+        compiler_params=pltpu.CompilerParams(vmem_limit_bytes=2 * 1024 * 1024),
     )(*held)
 
 
 def store(*refs):
-    copies = [
-        pltpu.make_async_copy(refs[k], refs[4 + k], refs[8].at[k]) for k in range(4)
-    ]
-    for copy in copies:
-        copy.start()
-    for copy in copies:
-        copy.wait()
+    whole, done = refs[8:]
+    for k in range(4):
+        pltpu.make_async_copy(refs[k], refs[4 + k], done.at[0]).start()
+    pltpu.make_async_copy(whole, whole, done.at[0]).wait()
 
 
 def solution(mesh):

time: 13.3 us -> 13.3 us (level)
  no operation moved by 1% of the time
where the time goes in v6:
time: 13.3 us; the launch traced here: 13.1 us
  Pallas kernels  12.4 us (93%)
  between operations  0.64 us (5%)
    pallas_call x1, Pallas kernels, shards(): pl.pallas_call(functools.partial(kernel, rows, owners), out_shape=tuple((...  11.8 us
    pallas_call x1, Pallas kernels, shards(): pl.pallas_call(store, out_shape=results, in_specs=[vmem] * 4, out_specs=(...  0.69 us

profile of v6, /device:TPU:1, one launch (start us, length us, event | category | flops | bytes accessed | tf_op | source)
XLA Modules:
  0.0 13.1 jit_solution(17856531540306038249)
XLA Ops:
  0.6 11.8 %shard_map.147 = (f32[3,6,8,128]{3,2,1,0:T(8,128)S(1)}, f32[3,6,8,128]{3,2,1,0:T(8,128)S(1)}, f32[64,128]{1,0:T(8,128)S(1)}, f32[64,128]{1,0:T(8,128)S(1)}) custom-call(f32[18,8,128]{2,1,0:T(8,128)} %bitcast.9, f32[144,128]{1,0:T(8,128)} %bitcast.10, f32[6,8,128]{2,1,0:T(8,128)} %lam_hbm.1, f32[6,8,128]{2,1,0:T(8,128)} %mu_hbm.1, f32[48,128]{1,0:T(8,128)} %bitcast.11, ...), custom_call_target="tpu_custom_call" | custom-call | tf_op jit(solution)/shard_map/pallas_call | solution.py:749
  12.4 0.7 %shard_map.148 = (f32[3,6,8,128]{3,2,1,0:T(8,128)}, f32[3,6,8,128]{3,2,1,0:T(8,128)}, f32[64,128]{1,0:T(8,128)}, f32[64,128]{1,0:T(8,128)}) custom-call(f32[3,6,8,128]{3,2,1,0:T(8,128)S(1)} %get-tuple-element.8.refs_0_, f32[3,6,8,128]{3,2,1,0:T(8,128)S(1)} %get-tuple-element.9.refs_1_, f32[64,128]{1,0:T(8,128)S(1)} %get-tuple-element.10.refs_2_, ...), custom_call_target="tpu_custom_call" | custom-call | tf_op jit(solution)/shard_map/pallas_call | solution.py:786

commit v7 on v6

--- a/solution.py
+++ b/solution.py
@@ -161,6 +161,7 @@
     frame_ref,
     near_ref,
     wide_ref,
+    far_ref,
     arch_ref,
     counts_ref,
     cells_ref,
@@ -243,16 +244,8 @@
 
     start_load("cells", cells_ref, (("cells", cells_hbm),))
     start_load("counts", counts_ref, (("counts", counts_hbm),))
-    start_load(
-        "wide",
-        wide_ref,
-        (
-            ("buoy", buoy_hbm),
-            ("stiff", stiff_hbm),
-            ("q_prev", q_prev_hbm),
-            ("u_prev", u_prev_hbm),
-        ),
-    )
+    start_load("far", far_ref, (("u_prev", u_prev_hbm), ("buoy", buoy_hbm)))
+    start_load("wide", wide_ref, (("stiff", stiff_hbm), ("q_prev", q_prev_hbm)))
 
     def half(ref, dx):
         return ref if dx == 0 else ref.at[pl.ds(RIM if dx > 0 else 0, RIM)]
@@ -553,7 +546,7 @@
     base = surface_motion(u)
     home_base = [group_sum(c, base) for c in range(3)]
 
-    gain = load("buoy")[...].reshape(nz, 8, 128) * dt2
+    gain = load("buoy")[...] * dt2
     overlap_left, overlap_right = [], []
     for x in range(8):
         there = live & ((corner_x == float(x)) | (corner_x == float(x - 1)))
@@ -728,10 +721,10 @@
     tiles = (3 * nz, 8, 128)
     operands = (
         u_now.reshape(tiles),
-        u_prev.reshape(3 * nz * 8, 128),
+        u_prev.reshape(tiles),
         lame_lambda,
         lame_mu,
-        buoyancy.reshape(nz * 8, 128),
+        buoyancy,
         q_now,
         q_prev,
         archetype.reshape(1, slots),
@@ -770,11 +763,12 @@
         + [
             pltpu.VMEM((slots + 3 * kinds, freedoms), F32),
             pltpu.VMEM((5 * nz, 8, 128), F32),
-            pltpu.VMEM((kinds * freedoms + slots + 4 * nz * 8, freedoms), F32),
+            pltpu.VMEM((kinds * freedoms + slots, freedoms), F32),
+            pltpu.VMEM((4 * nz, 8, 128), F32),
             pltpu.VMEM((1, slots), jnp.int32),
             pltpu.VMEM(counts.shape, jnp.int32),
             pltpu.VMEM(footprint.shape, jnp.int32),
-            dma((6,)),
+            dma((7,)),
             dma((1,)),
             dma((STEPS + 3,)),
             pltpu.SemaphoreType.REGULAR((len(HEARD) + owners - 2,)),

time: 13.3 us -> 13.3 us (level)
  no operation moved by 1% of the time
where the time goes in v7:
time: 13.3 us; the launch traced here: 13.1 us
  Pallas kernels  12.5 us (94%)
  between operations  0.64 us (5%)
    pallas_call x1, Pallas kernels, shards(): pl.pallas_call(functools.partial(kernel, rows, owners), out_shape=tuple((...  11.8 us
    pallas_call x1, Pallas kernels, shards(): pl.pallas_call(store, out_shape=results, in_specs=[vmem] * 4, out_specs=(...  0.69 us

profile of v7, /device:TPU:1, one launch (start us, length us, event | category | flops | bytes accessed | tf_op | source)
XLA Modules:
  0.0 13.1 jit_solution(16481241090324914468)
XLA Ops:
  0.6 11.8 %shard_map.147 = (f32[3,6,8,128]{3,2,1,0:T(8,128)S(1)}, f32[3,6,8,128]{3,2,1,0:T(8,128)S(1)}, f32[64,128]{1,0:T(8,128)S(1)}, f32[64,128]{1,0:T(8,128)S(1)}) custom-call(f32[18,8,128]{2,1,0:T(8,128)} %bitcast.8, f32[18,8,128]{2,1,0:T(8,128)} %bitcast.9, f32[6,8,128]{2,1,0:T(8,128)} %lam_hbm.1, f32[6,8,128]{2,1,0:T(8,128)} %mu_hbm.1, f32[6,8,128]{2,1,0:T(8,128)} %buoy_hbm.1, ...), custom_call_target="tpu_custom_call" | custom-call | tf_op jit(solution)/shard_map/pallas_call | solution.py:742
  12.4 0.7 %shard_map.148 = (f32[3,6,8,128]{3,2,1,0:T(8,128)}, f32[3,6,8,128]{3,2,1,0:T(8,128)}, f32[64,128]{1,0:T(8,128)}, f32[64,128]{1,0:T(8,128)}) custom-call(f32[3,6,8,128]{3,2,1,0:T(8,128)S(1)} %get-tuple-element.8.refs_0_, f32[3,6,8,128]{3,2,1,0:T(8,128)S(1)} %get-tuple-element.9.refs_1_, f32[64,128]{1,0:T(8,128)S(1)} %get-tuple-element.10.refs_2_, ...), custom_call_target="tpu_custom_call" | custom-call | tf_op jit(solution)/shard_map/pallas_call | solution.py:780
